TPU v7x, 32 devices: a whole 2x2x4 slice. The times are simulated.
32 devices in a mesh: grp: 2 (over x), dom: 4 (over y, core), test: 4 (over z).
Axes of the slice: x: 2, y: 2, z: 4, core: 2. Of those that a mesh axis runs over, the one named last changes fastest.
Arguments:
- log_conductivity: float32 [16, 32, 512], P('grp', 'dom'), parts along dimension 0, may hold values from -3 to 3
- storage: float32 [16, 32, 512], P('grp', 'dom'), parts along dimension 0, may hold values from 0.05 to 0.5
- recharge: float32 [16, 32, 512], P('grp', 'dom'), parts along dimension 0, may hold values from -4 to 4
- pump_cells: int32 [8], P(('grp', 'test')), parts along dimension 0, may hold values from 0 to 131071
- obs_cells: int32 [8, 32], P(('grp', 'test')), parts along dimension 0, may hold values from 0 to 131071
- obs_heads: float32 [8, 32], P(('grp', 'test')), parts along dimension 0, may hold values from -4 to 4
Outputs:
- gradient: float32 [16, 32, 512], P(('grp', 'test'), 'dom'), parts along dimension 0
- step_field: float32 [16, 32, 512], P(('grp', 'test'), 'dom'), parts along dimension 0
There are 2 independent parts, one for each index of `grp`. A program takes and returns all parts, laid end to end along the dimension named above; each array names one. Nothing has to cross between parts.
Inputs may be any that keep to these rules, and one draw needn't show every extreme that they name: `pump_cells`: flat index 32 * 512 * z + 512 * x + y of the pumping well's cell. `obs_cells`: flat index 32 * 512 * z + 512 * x + y of each port's cell; ports may repeat.
All inputs are finite; a program needn't handle non-finite values.
Results may differ from a plain program's by a relative error of at most 0.00027.
Values sent between devices are 32-bit elements; how exact they have to be, the bound alone decides.
A program may use at most 64 MiB of HBM per device.

v0:
```python
import math

import jax
import jax.numpy as jnp
from jax import lax
from jax.sharding import PartitionSpec as P

ITERS = 32
CORR = 16


LOW = 0.1
HIGH = 2.0
PUMP_RATE = 8.0
NOISE_VAR = 0.01
NUGGET = 1.0
SMOOTH = 2.0
HIGHEST = lax.Precision.HIGHEST


def padded_2(cells, sides, width):
    for axis, dim in sides:
        count = lax.axis_size(axis)
        ends = count - 1
        head = lax.slice_in_dim(cells, 0, width, axis=dim)
        tail = lax.slice_in_dim(cells, cells.shape[dim] - width, cells.shape[dim], axis=dim)
        cells = jnp.concatenate(
            [
                lax.ppermute(tail, axis, [(i, (i + 1) % count) for i in range(ends)]),
                cells,
                lax.ppermute(head, axis, [((i + 1) % count, i) for i in range(ends)]),
            ],
            axis=dim,
        )
    return cells


def chebyshev(rhs_field, apply_op, inverse_diag):
    centre_eig = 0.5 * (HIGH + LOW)
    half_span = 0.5 * (HIGH - LOW)
    ratio_eig = centre_eig / half_span
    rho_old = 1.0 / ratio_eig
    keep_list = []
    step_list = []
    for count_index in range(ITERS):
        rho_new = 1.0 / (2.0 * ratio_eig - rho_old)
        keep_list.append(rho_new * rho_old)
        step_list.append(2.0 * rho_new / half_span)
        rho_old = rho_new
    keep_table = jnp.array(keep_list, jnp.float32)
    step_table = jnp.array(step_list, jnp.float32)
    direction = inverse_diag * rhs_field / centre_eig

    def sweep_body(sweep_index, carry):
        residual, direction, iterate = carry
        residual = residual - apply_op(direction)
        direction = keep_table[sweep_index] * direction + step_table[sweep_index] * (
            inverse_diag * residual
        )
        iterate = iterate + direction
        return (residual, direction, iterate)

    final = lax.fori_loop(0, ITERS, sweep_body, (rhs_field, direction, direction))
    return final[2]


def prior_weight(freq_x_index, full_x, freq_y_index, full_y):
    wave_x = ((freq_x_index + full_x // 2) % full_x - full_x // 2).astype(jnp.float32) * (
        2.0 * math.pi / full_x
    )
    wave_y = ((freq_y_index + full_y // 2) % full_y - full_y // 2).astype(jnp.float32) * (
        2.0 * math.pi / full_y
    )
    wave_sq = wave_x[:, None] ** 2 + wave_y[None, :] ** 2
    return NUGGET + SMOOTH * CORR**2 / (1.0 + CORR**2 * wave_sq) ** 2


def trig_table(first_index, second_index, length):
    angles = (
        2.0
        * math.pi
        / length
        * (first_index[:, None] * second_index[None, :] % length).astype(jnp.float32)
    )
    return (jnp.cos(angles), jnp.sin(angles))


def widen(values):
    return jnp.stack([padded_2(values[0], (("dom", 1),), 1)])


def shards(log_conductivity, storage, recharge, pump_cells, obs_cells, obs_heads):
    depth_z, slab_x, width_y = log_conductivity.shape
    dom_count = lax.axis_size("dom")
    dom_index = lax.axis_index("dom")
    full_x = slab_x * dom_count
    test_count = pump_cells.shape[0]
    cell_count = depth_z * slab_x * width_y
    conduct = jnp.exp(log_conductivity)
    cond_wide = padded_2(conduct, (("dom", 1),), 1)
    cond_pad = jnp.pad(cond_wide, ((1, 1), (0, 0), (1, 1)))
    face_z = 0.5 * (cond_pad[:-1, 1:-1, 1:-1] + cond_pad[1:, 1:-1, 1:-1])
    face_x = 0.5 * (cond_pad[1:-1, :-1, 1:-1] + cond_pad[1:-1, 1:, 1:-1])
    face_y = 0.5 * (cond_pad[1:-1, 1:-1, :-1] + cond_pad[1:-1, 1:-1, 1:])
    diagonal = (
        storage
        + face_z[:-1]
        + face_z[1:]
        + face_x[:, :-1]
        + face_x[:, 1:]
        + face_y[:, :, :-1]
        + face_y[:, :, 1:]
    )
    inverse_diag = 1.0 / diagonal

    def apply_op(values):
        widened = widen(values)
        padded = jnp.pad(widened, ((0, 0), (1, 1), (0, 0), (1, 1)))
        result = storage * values
        result = (
            result
            + face_z[:-1] * (values - padded[:, :-2, 1:-1, 1:-1])
            + face_z[1:] * (values - padded[:, 2:, 1:-1, 1:-1])
        )
        result = (
            result
            + face_x[:, :-1] * (values - padded[:, 1:-1, :-2, 1:-1])
            + face_x[:, 1:] * (values - padded[:, 1:-1, 2:, 1:-1])
        )
        result = (
            result
            + face_y[:, :, :-1] * (values - padded[:, 1:-1, 1:-1, :-2])
            + face_y[:, :, 1:] * (values - padded[:, 1:-1, 1:-1, 2:])
        )
        return result

    def local_index(flat_cell):
        plane_size = full_x * width_y
        z_index = flat_cell // plane_size
        remainder = flat_cell % plane_size
        x_index = remainder // width_y - dom_index * slab_x
        y_index = remainder % width_y
        inside = (x_index >= 0) & (x_index < slab_x)
        return (inside, z_index * (slab_x * width_y) + x_index * width_y + y_index)

    test_offset = jnp.arange(test_count, dtype=jnp.int32) * cell_count
    total_cells = test_count * cell_count
    pump_inside, pump_local = local_index(pump_cells)
    pump_index = jnp.where(pump_inside, pump_local + test_offset, total_cells)
    obs_inside, obs_local = local_index(obs_cells)
    obs_index = jnp.where(obs_inside, obs_local + test_offset[:, None], total_cells)
    pumping = jnp.zeros((total_cells,), jnp.float32).at[pump_index].add(-PUMP_RATE, mode="drop")
    source = recharge[None] + pumping.reshape(test_count, depth_z, slab_x, width_y)
    head_field = chebyshev(source, apply_op, inverse_diag)
    observed = head_field.reshape(-1).at[obs_index].get(mode="fill", fill_value=0.0)
    misfit = (observed - obs_heads) / NOISE_VAR
    adjoint_src = jnp.zeros((total_cells,), jnp.float32).at[obs_index].add(misfit, mode="drop")
    adjoint = chebyshev(
        adjoint_src.reshape(test_count, depth_z, slab_x, width_y), apply_op, inverse_diag
    )
    stacked = jnp.stack([head_field, adjoint])
    both_wide = padded_2(stacked, (("dom", 3),), 1)
    both_pad = jnp.pad(both_wide, ((0, 0), (0, 0), (1, 1), (0, 0), (1, 1)))
    head_pad = both_pad[0]
    adj_pad = both_pad[1]
    products = (adjoint - adj_pad[:, :-2, 1:-1, 1:-1]) * (head_field - head_pad[:, :-2, 1:-1, 1:-1])
    products = products + (adjoint - adj_pad[:, 2:, 1:-1, 1:-1]) * (
        head_field - head_pad[:, 2:, 1:-1, 1:-1]
    )
    products = products + (adjoint - adj_pad[:, 1:-1, :-2, 1:-1]) * (
        head_field - head_pad[:, 1:-1, :-2, 1:-1]
    )
    products = products + (adjoint - adj_pad[:, 1:-1, 2:, 1:-1]) * (
        head_field - head_pad[:, 1:-1, 2:, 1:-1]
    )
    products = products + (adjoint - adj_pad[:, 1:-1, 1:-1, :-2]) * (
        head_field - head_pad[:, 1:-1, 1:-1, :-2]
    )
    products = products + (adjoint - adj_pad[:, 1:-1, 1:-1, 2:]) * (
        head_field - head_pad[:, 1:-1, 1:-1, 2:]
    )
    partial_grad = -0.5 * conduct * jnp.sum(products, axis=0)
    gradient = lax.psum_scatter(partial_grad, "test", scatter_dimension=0, tiled=True)
    layer_count = gradient.shape[0]
    y_range = jnp.arange(width_y, dtype=jnp.int32)
    cosine_y, sine_y = trig_table(y_range, y_range, width_y)
    flat_grad = gradient.reshape(layer_count * slab_x, width_y)
    real_y = jnp.dot(flat_grad, cosine_y, precision=HIGHEST, preferred_element_type=jnp.float32)
    imag_y = -jnp.dot(flat_grad, sine_y, precision=HIGHEST, preferred_element_type=jnp.float32)
    spectral_y = jnp.stack(
        [real_y.reshape(layer_count, slab_x, width_y), imag_y.reshape(layer_count, slab_x, width_y)]
    )
    regrouped = lax.all_to_all(spectral_y, "dom", split_axis=3, concat_axis=2, tiled=True)
    nx_full = regrouped.shape[2]
    y_local = regrouped.shape[3]
    x_range = jnp.arange(nx_full, dtype=jnp.int32)
    cosine_x, sine_x = trig_table(x_range, x_range, nx_full)
    real_part = regrouped[0]
    imag_part = regrouped[1]
    freq_re = jnp.einsum("fx,mxk->mfk", cosine_x, real_part, precision=HIGHEST) + jnp.einsum(
        "fx,mxk->mfk", sine_x, imag_part, precision=HIGHEST
    )
    freq_im = jnp.einsum("fx,mxk->mfk", cosine_x, imag_part, precision=HIGHEST) - jnp.einsum(
        "fx,mxk->mfk", sine_x, real_part, precision=HIGHEST
    )
    y_freq = dom_index * y_local + jnp.arange(y_local, dtype=jnp.int32)
    weights = prior_weight(x_range, nx_full, y_freq, width_y)
    freq_re = freq_re * weights
    freq_im = freq_im * weights
    back_re = (
        jnp.einsum("fx,mfk->mxk", cosine_x, freq_re, precision=HIGHEST)
        - jnp.einsum("fx,mfk->mxk", sine_x, freq_im, precision=HIGHEST)
    ) / nx_full
    back_im = (
        jnp.einsum("fx,mfk->mxk", cosine_x, freq_im, precision=HIGHEST)
        + jnp.einsum("fx,mfk->mxk", sine_x, freq_re, precision=HIGHEST)
    ) / nx_full
    returned = lax.all_to_all(
        jnp.stack([back_re, back_im]), "dom", split_axis=2, concat_axis=3, tiled=True
    )
    final_re = returned[0]
    final_im = returned[1]
    out_re = jnp.dot(
        final_re.reshape(layer_count * slab_x, width_y),
        cosine_y,
        precision=HIGHEST,
        preferred_element_type=jnp.float32,
    )
    out_im = jnp.dot(
        final_im.reshape(layer_count * slab_x, width_y),
        sine_y,
        precision=HIGHEST,
        preferred_element_type=jnp.float32,
    )
    step_field = ((out_re - out_im) / width_y).reshape(layer_count, slab_x, width_y)
    return (gradient, step_field)


def solution(mesh):
    in_specs = (
        P("grp", "dom", None),
        P("grp", "dom", None),
        P("grp", "dom", None),
        P(("grp", "test")),
        P(("grp", "test"), None),
        P(("grp", "test"), None),
    )
    out_specs = (P(("grp", "test"), "dom", None), P(("grp", "test"), "dom", None))
    return jax.shard_map(shards, mesh=mesh, in_specs=in_specs, out_specs=out_specs, check_vma=False)
```

profile of v0, /device:TPU:0, one launch (start us, length us, event | category | flops | bytes accessed | tf_op | source)
XLA Modules:
  0.0 652.8 jit_solution(18090845809103112659)
XLA Ops:
  18.1 275.3 %while.41 = (s32[]{:T(128)}, f32[1,8,8,512]{3,2,1,0:T(8,128)S(1)}, f32[1,8,8,512]{3,2,1,0:T(8,128)S(1)}, f32[1,8,8,512]{3,2,1,0:T(8,128)S(1)}, f32[8,8,512]{2,1,...) while((s32[]{:T(128)}, f32[1,8,8,512]{3,2,1,0:T(8,128)S(1)}, ...), condition=%wide.region_1.2_spmd.clone, body=%wide.region_0.1_spmd.sunk.clone.sunk | while | flops 901122 | bytes 2883813 | solution.py:63
  19.4 5.2 collective-permute-start.1
  37.2 4.4 collective-permute-start.1
  45.8 4.4 collective-permute-start.1
  63.0 4.4 collective-permute-start.1
  71.6 4.4 collective-permute-start.1
  80.1 4.4 collective-permute-start.1
  88.7 4.4 collective-permute-start.1
  97.3 4.4 collective-permute-start.1
  114.5 4.4 collective-permute-start.1
  123.1 4.4 collective-permute-start.1
  131.7 4.4 collective-permute-start.1
  140.2 4.4 collective-permute-start.1
  148.8 4.4 collective-permute-start.1
  166.0 4.4 collective-permute-start.1
  174.6 4.4 collective-permute-start.1
  183.2 4.4 collective-permute-start.1
  191.7 4.4 collective-permute-start.1
  200.3 4.4 collective-permute-start.1
  208.9 4.4 collective-permute-start.1
  226.1 4.4 collective-permute-start.1
  234.7 4.4 collective-permute-start.1
  243.3 4.4 collective-permute-start.1
  251.8 4.4 collective-permute-start.1
  260.4 4.4 collective-permute-start.1
  277.6 4.4 collective-permute-start.1
  286.2 4.4 collective-permute-start.1
  295.1 275.6 %while.42 = (s32[]{:T(128)}, f32[1,8,8,512]{3,2,1,0:T(8,128)S(1)}, f32[1,8,8,512]{3,2,1,0:T(8,128)S(1)}, f32[1,8,8,512]{3,2,1,0:T(8,128)S(1)}, f32[8,8,512]{2,1,...) while((s32[]{:T(128)}, f32[1,8,8,512]{3,2,1,0:T(8,128)S(1)}, ...), condition=%wide.region_4.5_spmd.clone, body=%wide.region_3.4_spmd.sunk.clone.sunk | while | flops 901122 | bytes 2883813 | solution.py:63
  313.6 4.5 collective-permute-start.3
  322.2 4.5 collective-permute-start.3
  330.8 4.5 collective-permute-start.3
  339.5 4.5 collective-permute-start.3
  348.1 4.5 collective-permute-start.3
  356.7 4.5 collective-permute-start.3
  365.3 4.5 collective-permute-start.3
  373.9 4.5 collective-permute-start.3
  382.5 4.5 collective-permute-start.3
  391.1 4.5 collective-permute-start.3
  399.8 4.5 collective-permute-start.3
  408.4 4.5 collective-permute-start.3
  417.0 4.5 collective-permute-start.3
  425.6 4.5 collective-permute-start.3
  434.2 4.5 collective-permute-start.3
  442.8 4.5 collective-permute-start.3
  451.5 4.5 collective-permute-start.3
  460.1 4.5 collective-permute-start.3
  468.7 4.5 collective-permute-start.3
  477.3 4.5 collective-permute-start.3
  485.9 4.5 collective-permute-start.3
  494.5 4.5 collective-permute-start.3
  503.1 4.5 collective-permute-start.3
  511.8 4.5 collective-permute-start.3
  520.4 4.5 collective-permute-start.3
  529.0 4.5 collective-permute-start.3
  537.6 4.5 collective-permute-start.3
  546.2 4.5 collective-permute-start.3
  554.8 4.5 collective-permute-start.3
  563.5 4.5 collective-permute-start.3
  581.6 21.9 %reduce-scatter.2.cloned.1.call-done = f32[2,8,512]{2,1,0:T(8,128)} async-done(((f32[8,8,512]{2,1,0:T(8,128)}), f32[2,8,512]{2,1,0:T(8,128)}) %reduce-scatter.2.cloned.1.call-update) | async-done | bytes 32784 | tf_op jit(solution)/shard_map/reduce_scatter | solution.py:183
  603.5 5.4 convolution_bitcast_fusion
  608.9 4.6 fusion.48
  629.7 6.5 all_to_all.30
  636.2 4.5 fusion.61
  640.7 5.2 fusion.39
  (594 shorter events, 336.2 us)
Async XLA Ops:
  7.2 596.3 %reduce-scatter.2.cloned.1.call-start = ((), (), s32[]{:S(2)}) async-start(), calls=%async_computation.3 | async-start | bytes 163840 | tf_op jit(solution)/shard_map/reduce_scatter | solution.py:183
  8.2 7.0 %collective-permute-start.4 = (f32[8,1,512]{2,1,0:T(1,128)S(1)}, f32[8,1,512]{2,1,0:T(1,128)S(1)}, u32[]{:S(2)}, u32[]{:S(2)}) collective-permute-start(f32[8,1,512]{2,1,0:T(1,128)S(1)} %get-tuple-element.661), channel_id=1, source_target_pairs={{0,4},{4,8},{8,12},{1,5},{5,9},{9,13},{2,6},{6,10},{10,14},{3,7},{... | collective-permute-start | bytes 49160 | tf_op jit(solution)/shard_map/ppermute | solution.py:29
  18.1 7.8 %collective-permute-start = (f32[8,1,512]{2,1,0:T(1,128)S(1)}, f32[8,1,512]{2,1,0:T(1,128)S(1)}, u32[]{:S(2)}, u32[]{:S(2)}) collective-permute-start(f32[8,1,512]{2,1,0:T(1,128)S(1)} %get-tuple-element.774), channel_id=1, source_target_pairs={{4,0},{8,4},{12,8},{5,1},{9,5},{13,9},{6,2},{10,6},{14,10},{7,3},{... | collective-permute-start | bytes 49160 | tf_op jit(solution)/shard_map/while/body/eval_jaxpr/ppermute | solution.py:31
  35.9 7.0 %collective-permute-start = (f32[8,1,512]{2,1,0:T(1,128)S(1)}, f32[8,1,512]{2,1,0:T(1,128)S(1)}, u32[]{:S(2)}, u32[]{:S(2)}) collective-permute-start(f32[8,1,512]{2,1,0:T(1,128)S(1)} %get-tuple-element.774), channel_id=1, source_target_pairs={{4,0},{8,4},{12,8},{5,1},{9,5},{13,9},{6,2},{10,6},{14,10},{7,3},{... | collective-permute-start | bytes 49160 | tf_op jit(solution)/shard_map/while/body/eval_jaxpr/ppermute | solution.py:31
  44.5 7.0 %collective-permute-start = (f32[8,1,512]{2,1,0:T(1,128)S(1)}, f32[8,1,512]{2,1,0:T(1,128)S(1)}, u32[]{:S(2)}, u32[]{:S(2)}) collective-permute-start(f32[8,1,512]{2,1,0:T(1,128)S(1)} %get-tuple-element.774), channel_id=1, source_target_pairs={{4,0},{8,4},{12,8},{5,1},{9,5},{13,9},{6,2},{10,6},{14,10},{7,3},{... | collective-permute-start | bytes 49160 | tf_op jit(solution)/shard_map/while/body/eval_jaxpr/ppermute | solution.py:31
  53.1 7.0 %collective-permute-start = (f32[8,1,512]{2,1,0:T(1,128)S(1)}, f32[8,1,512]{2,1,0:T(1,128)S(1)}, u32[]{:S(2)}, u32[]{:S(2)}) collective-permute-start(f32[8,1,512]{2,1,0:T(1,128)S(1)} %get-tuple-element.774), channel_id=1, source_target_pairs={{4,0},{8,4},{12,8},{5,1},{9,5},{13,9},{6,2},{10,6},{14,10},{7,3},{... | collective-permute-start | bytes 49160 | tf_op jit(solution)/shard_map/while/body/eval_jaxpr/ppermute | solution.py:31
  61.7 7.0 %collective-permute-start = (f32[8,1,512]{2,1,0:T(1,128)S(1)}, f32[8,1,512]{2,1,0:T(1,128)S(1)}, u32[]{:S(2)}, u32[]{:S(2)}) collective-permute-start(f32[8,1,512]{2,1,0:T(1,128)S(1)} %get-tuple-element.774), channel_id=1, source_target_pairs={{4,0},{8,4},{12,8},{5,1},{9,5},{13,9},{6,2},{10,6},{14,10},{7,3},{... | collective-permute-start | bytes 49160 | tf_op jit(solution)/shard_map/while/body/eval_jaxpr/ppermute | solution.py:31
  70.3 7.0 %collective-permute-start = (f32[8,1,512]{2,1,0:T(1,128)S(1)}, f32[8,1,512]{2,1,0:T(1,128)S(1)}, u32[]{:S(2)}, u32[]{:S(2)}) collective-permute-start(f32[8,1,512]{2,1,0:T(1,128)S(1)} %get-tuple-element.774), channel_id=1, source_target_pairs={{4,0},{8,4},{12,8},{5,1},{9,5},{13,9},{6,2},{10,6},{14,10},{7,3},{... | collective-permute-start | bytes 49160 | tf_op jit(solution)/shard_map/while/body/eval_jaxpr/ppermute | solution.py:31
  78.8 7.0 %collective-permute-start = (f32[8,1,512]{2,1,0:T(1,128)S(1)}, f32[8,1,512]{2,1,0:T(1,128)S(1)}, u32[]{:S(2)}, u32[]{:S(2)}) collective-permute-start(f32[8,1,512]{2,1,0:T(1,128)S(1)} %get-tuple-element.774), channel_id=1, source_target_pairs={{4,0},{8,4},{12,8},{5,1},{9,5},{13,9},{6,2},{10,6},{14,10},{7,3},{... | collective-permute-start | bytes 49160 | tf_op jit(solution)/shard_map/while/body/eval_jaxpr/ppermute | solution.py:31
  87.4 7.0 %collective-permute-start = (f32[8,1,512]{2,1,0:T(1,128)S(1)}, f32[8,1,512]{2,1,0:T(1,128)S(1)}, u32[]{:S(2)}, u32[]{:S(2)}) collective-permute-start(f32[8,1,512]{2,1,0:T(1,128)S(1)} %get-tuple-element.774), channel_id=1, source_target_pairs={{4,0},{8,4},{12,8},{5,1},{9,5},{13,9},{6,2},{10,6},{14,10},{7,3},{... | collective-permute-start | bytes 49160 | tf_op jit(solution)/shard_map/while/body/eval_jaxpr/ppermute | solution.py:31
  96.0 7.0 %collective-permute-start = (f32[8,1,512]{2,1,0:T(1,128)S(1)}, f32[8,1,512]{2,1,0:T(1,128)S(1)}, u32[]{:S(2)}, u32[]{:S(2)}) collective-permute-start(f32[8,1,512]{2,1,0:T(1,128)S(1)} %get-tuple-element.774), channel_id=1, source_target_pairs={{4,0},{8,4},{12,8},{5,1},{9,5},{13,9},{6,2},{10,6},{14,10},{7,3},{... | collective-permute-start | bytes 49160 | tf_op jit(solution)/shard_map/while/body/eval_jaxpr/ppermute | solution.py:31
  104.6 7.0 %collective-permute-start = (f32[8,1,512]{2,1,0:T(1,128)S(1)}, f32[8,1,512]{2,1,0:T(1,128)S(1)}, u32[]{:S(2)}, u32[]{:S(2)}) collective-permute-start(f32[8,1,512]{2,1,0:T(1,128)S(1)} %get-tuple-element.774), channel_id=1, source_target_pairs={{4,0},{8,4},{12,8},{5,1},{9,5},{13,9},{6,2},{10,6},{14,10},{7,3},{... | collective-permute-start | bytes 49160 | tf_op jit(solution)/shard_map/while/body/eval_jaxpr/ppermute | solution.py:31
  113.2 7.0 %collective-permute-start = (f32[8,1,512]{2,1,0:T(1,128)S(1)}, f32[8,1,512]{2,1,0:T(1,128)S(1)}, u32[]{:S(2)}, u32[]{:S(2)}) collective-permute-start(f32[8,1,512]{2,1,0:T(1,128)S(1)} %get-tuple-element.774), channel_id=1, source_target_pairs={{4,0},{8,4},{12,8},{5,1},{9,5},{13,9},{6,2},{10,6},{14,10},{7,3},{... | collective-permute-start | bytes 49160 | tf_op jit(solution)/shard_map/while/body/eval_jaxpr/ppermute | solution.py:31
  121.8 7.0 %collective-permute-start = (f32[8,1,512]{2,1,0:T(1,128)S(1)}, f32[8,1,512]{2,1,0:T(1,128)S(1)}, u32[]{:S(2)}, u32[]{:S(2)}) collective-permute-start(f32[8,1,512]{2,1,0:T(1,128)S(1)} %get-tuple-element.774), channel_id=1, source_target_pairs={{4,0},{8,4},{12,8},{5,1},{9,5},{13,9},{6,2},{10,6},{14,10},{7,3},{... | collective-permute-start | bytes 49160 | tf_op jit(solution)/shard_map/while/body/eval_jaxpr/ppermute | solution.py:31
  130.4 7.0 %collective-permute-start = (f32[8,1,512]{2,1,0:T(1,128)S(1)}, f32[8,1,512]{2,1,0:T(1,128)S(1)}, u32[]{:S(2)}, u32[]{:S(2)}) collective-permute-start(f32[8,1,512]{2,1,0:T(1,128)S(1)} %get-tuple-element.774), channel_id=1, source_target_pairs={{4,0},{8,4},{12,8},{5,1},{9,5},{13,9},{6,2},{10,6},{14,10},{7,3},{... | collective-permute-start | bytes 49160 | tf_op jit(solution)/shard_map/while/body/eval_jaxpr/ppermute | solution.py:31
  138.9 7.0 %collective-permute-start = (f32[8,1,512]{2,1,0:T(1,128)S(1)}, f32[8,1,512]{2,1,0:T(1,128)S(1)}, u32[]{:S(2)}, u32[]{:S(2)}) collective-permute-start(f32[8,1,512]{2,1,0:T(1,128)S(1)} %get-tuple-element.774), channel_id=1, source_target_pairs={{4,0},{8,4},{12,8},{5,1},{9,5},{13,9},{6,2},{10,6},{14,10},{7,3},{... | collective-permute-start | bytes 49160 | tf_op jit(solution)/shard_map/while/body/eval_jaxpr/ppermute | solution.py:31
  147.5 7.0 %collective-permute-start = (f32[8,1,512]{2,1,0:T(1,128)S(1)}, f32[8,1,512]{2,1,0:T(1,128)S(1)}, u32[]{:S(2)}, u32[]{:S(2)}) collective-permute-start(f32[8,1,512]{2,1,0:T(1,128)S(1)} %get-tuple-element.774), channel_id=1, source_target_pairs={{4,0},{8,4},{12,8},{5,1},{9,5},{13,9},{6,2},{10,6},{14,10},{7,3},{... | collective-permute-start | bytes 49160 | tf_op jit(solution)/shard_map/while/body/eval_jaxpr/ppermute | solution.py:31
  156.1 7.0 %collective-permute-start = (f32[8,1,512]{2,1,0:T(1,128)S(1)}, f32[8,1,512]{2,1,0:T(1,128)S(1)}, u32[]{:S(2)}, u32[]{:S(2)}) collective-permute-start(f32[8,1,512]{2,1,0:T(1,128)S(1)} %get-tuple-element.774), channel_id=1, source_target_pairs={{4,0},{8,4},{12,8},{5,1},{9,5},{13,9},{6,2},{10,6},{14,10},{7,3},{... | collective-permute-start | bytes 49160 | tf_op jit(solution)/shard_map/while/body/eval_jaxpr/ppermute | solution.py:31
  164.7 7.0 %collective-permute-start = (f32[8,1,512]{2,1,0:T(1,128)S(1)}, f32[8,1,512]{2,1,0:T(1,128)S(1)}, u32[]{:S(2)}, u32[]{:S(2)}) collective-permute-start(f32[8,1,512]{2,1,0:T(1,128)S(1)} %get-tuple-element.774), channel_id=1, source_target_pairs={{4,0},{8,4},{12,8},{5,1},{9,5},{13,9},{6,2},{10,6},{14,10},{7,3},{... | collective-permute-start | bytes 49160 | tf_op jit(solution)/shard_map/while/body/eval_jaxpr/ppermute | solution.py:31
  173.3 7.0 %collective-permute-start = (f32[8,1,512]{2,1,0:T(1,128)S(1)}, f32[8,1,512]{2,1,0:T(1,128)S(1)}, u32[]{:S(2)}, u32[]{:S(2)}) collective-permute-start(f32[8,1,512]{2,1,0:T(1,128)S(1)} %get-tuple-element.774), channel_id=1, source_target_pairs={{4,0},{8,4},{12,8},{5,1},{9,5},{13,9},{6,2},{10,6},{14,10},{7,3},{... | collective-permute-start | bytes 49160 | tf_op jit(solution)/shard_map/while/body/eval_jaxpr/ppermute | solution.py:31
  181.9 7.0 %collective-permute-start = (f32[8,1,512]{2,1,0:T(1,128)S(1)}, f32[8,1,512]{2,1,0:T(1,128)S(1)}, u32[]{:S(2)}, u32[]{:S(2)}) collective-permute-start(f32[8,1,512]{2,1,0:T(1,128)S(1)} %get-tuple-element.774), channel_id=1, source_target_pairs={{4,0},{8,4},{12,8},{5,1},{9,5},{13,9},{6,2},{10,6},{14,10},{7,3},{... | collective-permute-start | bytes 49160 | tf_op jit(solution)/shard_map/while/body/eval_jaxpr/ppermute | solution.py:31
  190.4 7.0 %collective-permute-start = (f32[8,1,512]{2,1,0:T(1,128)S(1)}, f32[8,1,512]{2,1,0:T(1,128)S(1)}, u32[]{:S(2)}, u32[]{:S(2)}) collective-permute-start(f32[8,1,512]{2,1,0:T(1,128)S(1)} %get-tuple-element.774), channel_id=1, source_target_pairs={{4,0},{8,4},{12,8},{5,1},{9,5},{13,9},{6,2},{10,6},{14,10},{7,3},{... | collective-permute-start | bytes 49160 | tf_op jit(solution)/shard_map/while/body/eval_jaxpr/ppermute | solution.py:31
  199.0 7.0 %collective-permute-start = (f32[8,1,512]{2,1,0:T(1,128)S(1)}, f32[8,1,512]{2,1,0:T(1,128)S(1)}, u32[]{:S(2)}, u32[]{:S(2)}) collective-permute-start(f32[8,1,512]{2,1,0:T(1,128)S(1)} %get-tuple-element.774), channel_id=1, source_target_pairs={{4,0},{8,4},{12,8},{5,1},{9,5},{13,9},{6,2},{10,6},{14,10},{7,3},{... | collective-permute-start | bytes 49160 | tf_op jit(solution)/shard_map/while/body/eval_jaxpr/ppermute | solution.py:31
  207.6 7.0 %collective-permute-start = (f32[8,1,512]{2,1,0:T(1,128)S(1)}, f32[8,1,512]{2,1,0:T(1,128)S(1)}, u32[]{:S(2)}, u32[]{:S(2)}) collective-permute-start(f32[8,1,512]{2,1,0:T(1,128)S(1)} %get-tuple-element.774), channel_id=1, source_target_pairs={{4,0},{8,4},{12,8},{5,1},{9,5},{13,9},{6,2},{10,6},{14,10},{7,3},{... | collective-permute-start | bytes 49160 | tf_op jit(solution)/shard_map/while/body/eval_jaxpr/ppermute | solution.py:31
  216.2 7.0 %collective-permute-start = (f32[8,1,512]{2,1,0:T(1,128)S(1)}, f32[8,1,512]{2,1,0:T(1,128)S(1)}, u32[]{:S(2)}, u32[]{:S(2)}) collective-permute-start(f32[8,1,512]{2,1,0:T(1,128)S(1)} %get-tuple-element.774), channel_id=1, source_target_pairs={{4,0},{8,4},{12,8},{5,1},{9,5},{13,9},{6,2},{10,6},{14,10},{7,3},{... | collective-permute-start | bytes 49160 | tf_op jit(solution)/shard_map/while/body/eval_jaxpr/ppermute | solution.py:31
  224.8 7.0 %collective-permute-start = (f32[8,1,512]{2,1,0:T(1,128)S(1)}, f32[8,1,512]{2,1,0:T(1,128)S(1)}, u32[]{:S(2)}, u32[]{:S(2)}) collective-permute-start(f32[8,1,512]{2,1,0:T(1,128)S(1)} %get-tuple-element.774), channel_id=1, source_target_pairs={{4,0},{8,4},{12,8},{5,1},{9,5},{13,9},{6,2},{10,6},{14,10},{7,3},{... | collective-permute-start | bytes 49160 | tf_op jit(solution)/shard_map/while/body/eval_jaxpr/ppermute | solution.py:31
  233.4 7.0 %collective-permute-start = (f32[8,1,512]{2,1,0:T(1,128)S(1)}, f32[8,1,512]{2,1,0:T(1,128)S(1)}, u32[]{:S(2)}, u32[]{:S(2)}) collective-permute-start(f32[8,1,512]{2,1,0:T(1,128)S(1)} %get-tuple-element.774), channel_id=1, source_target_pairs={{4,0},{8,4},{12,8},{5,1},{9,5},{13,9},{6,2},{10,6},{14,10},{7,3},{... | collective-permute-start | bytes 49160 | tf_op jit(solution)/shard_map/while/body/eval_jaxpr/ppermute | solution.py:31
  242.0 7.0 %collective-permute-start = (f32[8,1,512]{2,1,0:T(1,128)S(1)}, f32[8,1,512]{2,1,0:T(1,128)S(1)}, u32[]{:S(2)}, u32[]{:S(2)}) collective-permute-start(f32[8,1,512]{2,1,0:T(1,128)S(1)} %get-tuple-element.774), channel_id=1, source_target_pairs={{4,0},{8,4},{12,8},{5,1},{9,5},{13,9},{6,2},{10,6},{14,10},{7,3},{... | collective-permute-start | bytes 49160 | tf_op jit(solution)/shard_map/while/body/eval_jaxpr/ppermute | solution.py:31
  250.5 7.0 %collective-permute-start = (f32[8,1,512]{2,1,0:T(1,128)S(1)}, f32[8,1,512]{2,1,0:T(1,128)S(1)}, u32[]{:S(2)}, u32[]{:S(2)}) collective-permute-start(f32[8,1,512]{2,1,0:T(1,128)S(1)} %get-tuple-element.774), channel_id=1, source_target_pairs={{4,0},{8,4},{12,8},{5,1},{9,5},{13,9},{6,2},{10,6},{14,10},{7,3},{... | collective-permute-start | bytes 49160 | tf_op jit(solution)/shard_map/while/body/eval_jaxpr/ppermute | solution.py:31
  259.1 7.0 %collective-permute-start = (f32[8,1,512]{2,1,0:T(1,128)S(1)}, f32[8,1,512]{2,1,0:T(1,128)S(1)}, u32[]{:S(2)}, u32[]{:S(2)}) collective-permute-start(f32[8,1,512]{2,1,0:T(1,128)S(1)} %get-tuple-element.774), channel_id=1, source_target_pairs={{4,0},{8,4},{12,8},{5,1},{9,5},{13,9},{6,2},{10,6},{14,10},{7,3},{... | collective-permute-start | bytes 49160 | tf_op jit(solution)/shard_map/while/body/eval_jaxpr/ppermute | solution.py:31
  267.7 7.0 %collective-permute-start = (f32[8,1,512]{2,1,0:T(1,128)S(1)}, f32[8,1,512]{2,1,0:T(1,128)S(1)}, u32[]{:S(2)}, u32[]{:S(2)}) collective-permute-start(f32[8,1,512]{2,1,0:T(1,128)S(1)} %get-tuple-element.774), channel_id=1, source_target_pairs={{4,0},{8,4},{12,8},{5,1},{9,5},{13,9},{6,2},{10,6},{14,10},{7,3},{... | collective-permute-start | bytes 49160 | tf_op jit(solution)/shard_map/while/body/eval_jaxpr/ppermute | solution.py:31
  276.3 7.0 %collective-permute-start = (f32[8,1,512]{2,1,0:T(1,128)S(1)}, f32[8,1,512]{2,1,0:T(1,128)S(1)}, u32[]{:S(2)}, u32[]{:S(2)}) collective-permute-start(f32[8,1,512]{2,1,0:T(1,128)S(1)} %get-tuple-element.774), channel_id=1, source_target_pairs={{4,0},{8,4},{12,8},{5,1},{9,5},{13,9},{6,2},{10,6},{14,10},{7,3},{... | collective-permute-start | bytes 49160 | tf_op jit(solution)/shard_map/while/body/eval_jaxpr/ppermute | solution.py:31
  284.9 7.0 %collective-permute-start = (f32[8,1,512]{2,1,0:T(1,128)S(1)}, f32[8,1,512]{2,1,0:T(1,128)S(1)}, u32[]{:S(2)}, u32[]{:S(2)}) collective-permute-start(f32[8,1,512]{2,1,0:T(1,128)S(1)} %get-tuple-element.774), channel_id=1, source_target_pairs={{4,0},{8,4},{12,8},{5,1},{9,5},{13,9},{6,2},{10,6},{14,10},{7,3},{... | collective-permute-start | bytes 49160 | tf_op jit(solution)/shard_map/while/body/eval_jaxpr/ppermute | solution.py:31
  312.3 7.0 %collective-permute-start.2 = (f32[8,1,512]{2,1,0:T(1,128)S(1)}, f32[8,1,512]{2,1,0:T(1,128)S(1)}, u32[]{:S(2)}, u32[]{:S(2)}) collective-permute-start(f32[8,1,512]{2,1,0:T(1,128)S(1)} %get-tuple-element.788), channel_id=1, source_target_pairs={{4,0},{8,4},{12,8},{5,1},{9,5},{13,9},{6,2},{10,6},{14,10},{7,3},{... | collective-permute-start | bytes 49160 | tf_op jit(solution)/shard_map/while/body/eval_jaxpr/ppermute | solution.py:31
  320.9 7.0 %collective-permute-start.2 = (f32[8,1,512]{2,1,0:T(1,128)S(1)}, f32[8,1,512]{2,1,0:T(1,128)S(1)}, u32[]{:S(2)}, u32[]{:S(2)}) collective-permute-start(f32[8,1,512]{2,1,0:T(1,128)S(1)} %get-tuple-element.788), channel_id=1, source_target_pairs={{4,0},{8,4},{12,8},{5,1},{9,5},{13,9},{6,2},{10,6},{14,10},{7,3},{... | collective-permute-start | bytes 49160 | tf_op jit(solution)/shard_map/while/body/eval_jaxpr/ppermute | solution.py:31
  329.5 7.0 %collective-permute-start.2 = (f32[8,1,512]{2,1,0:T(1,128)S(1)}, f32[8,1,512]{2,1,0:T(1,128)S(1)}, u32[]{:S(2)}, u32[]{:S(2)}) collective-permute-start(f32[8,1,512]{2,1,0:T(1,128)S(1)} %get-tuple-element.788), channel_id=1, source_target_pairs={{4,0},{8,4},{12,8},{5,1},{9,5},{13,9},{6,2},{10,6},{14,10},{7,3},{... | collective-permute-start | bytes 49160 | tf_op jit(solution)/shard_map/while/body/eval_jaxpr/ppermute | solution.py:31
  338.2 7.0 %collective-permute-start.2 = (f32[8,1,512]{2,1,0:T(1,128)S(1)}, f32[8,1,512]{2,1,0:T(1,128)S(1)}, u32[]{:S(2)}, u32[]{:S(2)}) collective-permute-start(f32[8,1,512]{2,1,0:T(1,128)S(1)} %get-tuple-element.788), channel_id=1, source_target_pairs={{4,0},{8,4},{12,8},{5,1},{9,5},{13,9},{6,2},{10,6},{14,10},{7,3},{... | collective-permute-start | bytes 49160 | tf_op jit(solution)/shard_map/while/body/eval_jaxpr/ppermute | solution.py:31
  346.8 7.0 %collective-permute-start.2 = (f32[8,1,512]{2,1,0:T(1,128)S(1)}, f32[8,1,512]{2,1,0:T(1,128)S(1)}, u32[]{:S(2)}, u32[]{:S(2)}) collective-permute-start(f32[8,1,512]{2,1,0:T(1,128)S(1)} %get-tuple-element.788), channel_id=1, source_target_pairs={{4,0},{8,4},{12,8},{5,1},{9,5},{13,9},{6,2},{10,6},{14,10},{7,3},{... | collective-permute-start | bytes 49160 | tf_op jit(solution)/shard_map/while/body/eval_jaxpr/ppermute | solution.py:31
  355.4 7.0 %collective-permute-start.2 = (f32[8,1,512]{2,1,0:T(1,128)S(1)}, f32[8,1,512]{2,1,0:T(1,128)S(1)}, u32[]{:S(2)}, u32[]{:S(2)}) collective-permute-start(f32[8,1,512]{2,1,0:T(1,128)S(1)} %get-tuple-element.788), channel_id=1, source_target_pairs={{4,0},{8,4},{12,8},{5,1},{9,5},{13,9},{6,2},{10,6},{14,10},{7,3},{... | collective-permute-start | bytes 49160 | tf_op jit(solution)/shard_map/while/body/eval_jaxpr/ppermute | solution.py:31
  364.0 7.0 %collective-permute-start.2 = (f32[8,1,512]{2,1,0:T(1,128)S(1)}, f32[8,1,512]{2,1,0:T(1,128)S(1)}, u32[]{:S(2)}, u32[]{:S(2)}) collective-permute-start(f32[8,1,512]{2,1,0:T(1,128)S(1)} %get-tuple-element.788), channel_id=1, source_target_pairs={{4,0},{8,4},{12,8},{5,1},{9,5},{13,9},{6,2},{10,6},{14,10},{7,3},{... | collective-permute-start | bytes 49160 | tf_op jit(solution)/shard_map/while/body/eval_jaxpr/ppermute | solution.py:31
  372.6 7.0 %collective-permute-start.2 = (f32[8,1,512]{2,1,0:T(1,128)S(1)}, f32[8,1,512]{2,1,0:T(1,128)S(1)}, u32[]{:S(2)}, u32[]{:S(2)}) collective-permute-start(f32[8,1,512]{2,1,0:T(1,128)S(1)} %get-tuple-element.788), channel_id=1, source_target_pairs={{4,0},{8,4},{12,8},{5,1},{9,5},{13,9},{6,2},{10,6},{14,10},{7,3},{... | collective-permute-start | bytes 49160 | tf_op jit(solution)/shard_map/while/body/eval_jaxpr/ppermute | solution.py:31
  381.2 7.0 %collective-permute-start.2 = (f32[8,1,512]{2,1,0:T(1,128)S(1)}, f32[8,1,512]{2,1,0:T(1,128)S(1)}, u32[]{:S(2)}, u32[]{:S(2)}) collective-permute-start(f32[8,1,512]{2,1,0:T(1,128)S(1)} %get-tuple-element.788), channel_id=1, source_target_pairs={{4,0},{8,4},{12,8},{5,1},{9,5},{13,9},{6,2},{10,6},{14,10},{7,3},{... | collective-permute-start | bytes 49160 | tf_op jit(solution)/shard_map/while/body/eval_jaxpr/ppermute | solution.py:31
  389.8 7.0 %collective-permute-start.2 = (f32[8,1,512]{2,1,0:T(1,128)S(1)}, f32[8,1,512]{2,1,0:T(1,128)S(1)}, u32[]{:S(2)}, u32[]{:S(2)}) collective-permute-start(f32[8,1,512]{2,1,0:T(1,128)S(1)} %get-tuple-element.788), channel_id=1, source_target_pairs={{4,0},{8,4},{12,8},{5,1},{9,5},{13,9},{6,2},{10,6},{14,10},{7,3},{... | collective-permute-start | bytes 49160 | tf_op jit(solution)/shard_map/while/body/eval_jaxpr/ppermute | solution.py:31
  398.5 7.0 %collective-permute-start.2 = (f32[8,1,512]{2,1,0:T(1,128)S(1)}, f32[8,1,512]{2,1,0:T(1,128)S(1)}, u32[]{:S(2)}, u32[]{:S(2)}) collective-permute-start(f32[8,1,512]{2,1,0:T(1,128)S(1)} %get-tuple-element.788), channel_id=1, source_target_pairs={{4,0},{8,4},{12,8},{5,1},{9,5},{13,9},{6,2},{10,6},{14,10},{7,3},{... | collective-permute-start | bytes 49160 | tf_op jit(solution)/shard_map/while/body/eval_jaxpr/ppermute | solution.py:31
  407.1 7.0 %collective-permute-start.2 = (f32[8,1,512]{2,1,0:T(1,128)S(1)}, f32[8,1,512]{2,1,0:T(1,128)S(1)}, u32[]{:S(2)}, u32[]{:S(2)}) collective-permute-start(f32[8,1,512]{2,1,0:T(1,128)S(1)} %get-tuple-element.788), channel_id=1, source_target_pairs={{4,0},{8,4},{12,8},{5,1},{9,5},{13,9},{6,2},{10,6},{14,10},{7,3},{... | collective-permute-start | bytes 49160 | tf_op jit(solution)/shard_map/while/body/eval_jaxpr/ppermute | solution.py:31
  415.7 7.0 %collective-permute-start.2 = (f32[8,1,512]{2,1,0:T(1,128)S(1)}, f32[8,1,512]{2,1,0:T(1,128)S(1)}, u32[]{:S(2)}, u32[]{:S(2)}) collective-permute-start(f32[8,1,512]{2,1,0:T(1,128)S(1)} %get-tuple-element.788), channel_id=1, source_target_pairs={{4,0},{8,4},{12,8},{5,1},{9,5},{13,9},{6,2},{10,6},{14,10},{7,3},{... | collective-permute-start | bytes 49160 | tf_op jit(solution)/shard_map/while/body/eval_jaxpr/ppermute | solution.py:31
  424.3 7.0 %collective-permute-start.2 = (f32[8,1,512]{2,1,0:T(1,128)S(1)}, f32[8,1,512]{2,1,0:T(1,128)S(1)}, u32[]{:S(2)}, u32[]{:S(2)}) collective-permute-start(f32[8,1,512]{2,1,0:T(1,128)S(1)} %get-tuple-element.788), channel_id=1, source_target_pairs={{4,0},{8,4},{12,8},{5,1},{9,5},{13,9},{6,2},{10,6},{14,10},{7,3},{... | collective-permute-start | bytes 49160 | tf_op jit(solution)/shard_map/while/body/eval_jaxpr/ppermute | solution.py:31
  432.9 7.0 %collective-permute-start.2 = (f32[8,1,512]{2,1,0:T(1,128)S(1)}, f32[8,1,512]{2,1,0:T(1,128)S(1)}, u32[]{:S(2)}, u32[]{:S(2)}) collective-permute-start(f32[8,1,512]{2,1,0:T(1,128)S(1)} %get-tuple-element.788), channel_id=1, source_target_pairs={{4,0},{8,4},{12,8},{5,1},{9,5},{13,9},{6,2},{10,6},{14,10},{7,3},{... | collective-permute-start | bytes 49160 | tf_op jit(solution)/shard_map/while/body/eval_jaxpr/ppermute | solution.py:31
  441.5 7.0 %collective-permute-start.2 = (f32[8,1,512]{2,1,0:T(1,128)S(1)}, f32[8,1,512]{2,1,0:T(1,128)S(1)}, u32[]{:S(2)}, u32[]{:S(2)}) collective-permute-start(f32[8,1,512]{2,1,0:T(1,128)S(1)} %get-tuple-element.788), channel_id=1, source_target_pairs={{4,0},{8,4},{12,8},{5,1},{9,5},{13,9},{6,2},{10,6},{14,10},{7,3},{... | collective-permute-start | bytes 49160 | tf_op jit(solution)/shard_map/while/body/eval_jaxpr/ppermute | solution.py:31
  450.2 7.0 %collective-permute-start.2 = (f32[8,1,512]{2,1,0:T(1,128)S(1)}, f32[8,1,512]{2,1,0:T(1,128)S(1)}, u32[]{:S(2)}, u32[]{:S(2)}) collective-permute-start(f32[8,1,512]{2,1,0:T(1,128)S(1)} %get-tuple-element.788), channel_id=1, source_target_pairs={{4,0},{8,4},{12,8},{5,1},{9,5},{13,9},{6,2},{10,6},{14,10},{7,3},{... | collective-permute-start | bytes 49160 | tf_op jit(solution)/shard_map/while/body/eval_jaxpr/ppermute | solution.py:31
  458.8 7.0 %collective-permute-start.2 = (f32[8,1,512]{2,1,0:T(1,128)S(1)}, f32[8,1,512]{2,1,0:T(1,128)S(1)}, u32[]{:S(2)}, u32[]{:S(2)}) collective-permute-start(f32[8,1,512]{2,1,0:T(1,128)S(1)} %get-tuple-element.788), channel_id=1, source_target_pairs={{4,0},{8,4},{12,8},{5,1},{9,5},{13,9},{6,2},{10,6},{14,10},{7,3},{... | collective-permute-start | bytes 49160 | tf_op jit(solution)/shard_map/while/body/eval_jaxpr/ppermute | solution.py:31
  467.4 7.0 %collective-permute-start.2 = (f32[8,1,512]{2,1,0:T(1,128)S(1)}, f32[8,1,512]{2,1,0:T(1,128)S(1)}, u32[]{:S(2)}, u32[]{:S(2)}) collective-permute-start(f32[8,1,512]{2,1,0:T(1,128)S(1)} %get-tuple-element.788), channel_id=1, source_target_pairs={{4,0},{8,4},{12,8},{5,1},{9,5},{13,9},{6,2},{10,6},{14,10},{7,3},{... | collective-permute-start | bytes 49160 | tf_op jit(solution)/shard_map/while/body/eval_jaxpr/ppermute | solution.py:31
  476.0 7.0 %collective-permute-start.2 = (f32[8,1,512]{2,1,0:T(1,128)S(1)}, f32[8,1,512]{2,1,0:T(1,128)S(1)}, u32[]{:S(2)}, u32[]{:S(2)}) collective-permute-start(f32[8,1,512]{2,1,0:T(1,128)S(1)} %get-tuple-element.788), channel_id=1, source_target_pairs={{4,0},{8,4},{12,8},{5,1},{9,5},{13,9},{6,2},{10,6},{14,10},{7,3},{... | collective-permute-start | bytes 49160 | tf_op jit(solution)/shard_map/while/body/eval_jaxpr/ppermute | solution.py:31
  484.6 7.0 %collective-permute-start.2 = (f32[8,1,512]{2,1,0:T(1,128)S(1)}, f32[8,1,512]{2,1,0:T(1,128)S(1)}, u32[]{:S(2)}, u32[]{:S(2)}) collective-permute-start(f32[8,1,512]{2,1,0:T(1,128)S(1)} %get-tuple-element.788), channel_id=1, source_target_pairs={{4,0},{8,4},{12,8},{5,1},{9,5},{13,9},{6,2},{10,6},{14,10},{7,3},{... | collective-permute-start | bytes 49160 | tf_op jit(solution)/shard_map/while/body/eval_jaxpr/ppermute | solution.py:31
  493.2 7.0 %collective-permute-start.2 = (f32[8,1,512]{2,1,0:T(1,128)S(1)}, f32[8,1,512]{2,1,0:T(1,128)S(1)}, u32[]{:S(2)}, u32[]{:S(2)}) collective-permute-start(f32[8,1,512]{2,1,0:T(1,128)S(1)} %get-tuple-element.788), channel_id=1, source_target_pairs={{4,0},{8,4},{12,8},{5,1},{9,5},{13,9},{6,2},{10,6},{14,10},{7,3},{... | collective-permute-start | bytes 49160 | tf_op jit(solution)/shard_map/while/body/eval_jaxpr/ppermute | solution.py:31
  501.8 7.0 %collective-permute-start.2 = (f32[8,1,512]{2,1,0:T(1,128)S(1)}, f32[8,1,512]{2,1,0:T(1,128)S(1)}, u32[]{:S(2)}, u32[]{:S(2)}) collective-permute-start(f32[8,1,512]{2,1,0:T(1,128)S(1)} %get-tuple-element.788), channel_id=1, source_target_pairs={{4,0},{8,4},{12,8},{5,1},{9,5},{13,9},{6,2},{10,6},{14,10},{7,3},{... | collective-permute-start | bytes 49160 | tf_op jit(solution)/shard_map/while/body/eval_jaxpr/ppermute | solution.py:31
  510.5 7.0 %collective-permute-start.2 = (f32[8,1,512]{2,1,0:T(1,128)S(1)}, f32[8,1,512]{2,1,0:T(1,128)S(1)}, u32[]{:S(2)}, u32[]{:S(2)}) collective-permute-start(f32[8,1,512]{2,1,0:T(1,128)S(1)} %get-tuple-element.788), channel_id=1, source_target_pairs={{4,0},{8,4},{12,8},{5,1},{9,5},{13,9},{6,2},{10,6},{14,10},{7,3},{... | collective-permute-start | bytes 49160 | tf_op jit(solution)/shard_map/while/body/eval_jaxpr/ppermute | solution.py:31
  519.1 7.0 %collective-permute-start.2 = (f32[8,1,512]{2,1,0:T(1,128)S(1)}, f32[8,1,512]{2,1,0:T(1,128)S(1)}, u32[]{:S(2)}, u32[]{:S(2)}) collective-permute-start(f32[8,1,512]{2,1,0:T(1,128)S(1)} %get-tuple-element.788), channel_id=1, source_target_pairs={{4,0},{8,4},{12,8},{5,1},{9,5},{13,9},{6,2},{10,6},{14,10},{7,3},{... | collective-permute-start | bytes 49160 | tf_op jit(solution)/shard_map/while/body/eval_jaxpr/ppermute | solution.py:31
  527.7 7.0 %collective-permute-start.2 = (f32[8,1,512]{2,1,0:T(1,128)S(1)}, f32[8,1,512]{2,1,0:T(1,128)S(1)}, u32[]{:S(2)}, u32[]{:S(2)}) collective-permute-start(f32[8,1,512]{2,1,0:T(1,128)S(1)} %get-tuple-element.788), channel_id=1, source_target_pairs={{4,0},{8,4},{12,8},{5,1},{9,5},{13,9},{6,2},{10,6},{14,10},{7,3},{... | collective-permute-start | bytes 49160 | tf_op jit(solution)/shard_map/while/body/eval_jaxpr/ppermute | solution.py:31
  536.3 7.0 %collective-permute-start.2 = (f32[8,1,512]{2,1,0:T(1,128)S(1)}, f32[8,1,512]{2,1,0:T(1,128)S(1)}, u32[]{:S(2)}, u32[]{:S(2)}) collective-permute-start(f32[8,1,512]{2,1,0:T(1,128)S(1)} %get-tuple-element.788), channel_id=1, source_target_pairs={{4,0},{8,4},{12,8},{5,1},{9,5},{13,9},{6,2},{10,6},{14,10},{7,3},{... | collective-permute-start | bytes 49160 | tf_op jit(solution)/shard_map/while/body/eval_jaxpr/ppermute | solution.py:31
  544.9 7.0 %collective-permute-start.2 = (f32[8,1,512]{2,1,0:T(1,128)S(1)}, f32[8,1,512]{2,1,0:T(1,128)S(1)}, u32[]{:S(2)}, u32[]{:S(2)}) collective-permute-start(f32[8,1,512]{2,1,0:T(1,128)S(1)} %get-tuple-element.788), channel_id=1, source_target_pairs={{4,0},{8,4},{12,8},{5,1},{9,5},{13,9},{6,2},{10,6},{14,10},{7,3},{... | collective-permute-start | bytes 49160 | tf_op jit(solution)/shard_map/while/body/eval_jaxpr/ppermute | solution.py:31
  553.5 7.0 %collective-permute-start.2 = (f32[8,1,512]{2,1,0:T(1,128)S(1)}, f32[8,1,512]{2,1,0:T(1,128)S(1)}, u32[]{:S(2)}, u32[]{:S(2)}) collective-permute-start(f32[8,1,512]{2,1,0:T(1,128)S(1)} %get-tuple-element.788), channel_id=1, source_target_pairs={{4,0},{8,4},{12,8},{5,1},{9,5},{13,9},{6,2},{10,6},{14,10},{7,3},{... | collective-permute-start | bytes 49160 | tf_op jit(solution)/shard_map/while/body/eval_jaxpr/ppermute | solution.py:31
  562.2 7.0 %collective-permute-start.2 = (f32[8,1,512]{2,1,0:T(1,128)S(1)}, f32[8,1,512]{2,1,0:T(1,128)S(1)}, u32[]{:S(2)}, u32[]{:S(2)}) collective-permute-start(f32[8,1,512]{2,1,0:T(1,128)S(1)} %get-tuple-element.788), channel_id=1, source_target_pairs={{4,0},{8,4},{12,8},{5,1},{9,5},{13,9},{6,2},{10,6},{14,10},{7,3},{... | collective-permute-start | bytes 49160 | tf_op jit(solution)/shard_map/while/body/eval_jaxpr/ppermute | solution.py:31
  616.4 7.4 %all-to-all-start = ((f32[4,1,4096]{2,1,0:T(1,128)}), f32[4,1,4096]{2,1,0:T(1,128)S(1)}, u32[]{:S(2)}, u32[]{:S(2)}) async-start(f32[4,1,4096]{2,1,0:T(1,128)} %reshape.195), calls=%async_computation.1 | async-start | bytes 131072 | tf_op jit(solution)/shard_map/all_to_all | solution.py:193
  (78 other events, 410.8 us)
Sparse Core Ops, SparseCore 0:
  581.7 21.7 reduce-scatter.1
where the time goes:
time: 658 us; the launch traced here: 653 us
  starting transfers between devices  380 us (58%)
  other arithmetic  105 us (16%)
  local copies, waits for them, and re-layouts  90.5 us (14%)
  waiting for transfers between devices  29.8 us (5%)
  matrix products  21.9 us (3%)
  between operations  15.6 us (2%)
    ppermute x66, starting transfers between devices, padded_2(): lax.ppermute(tail, axis, [(i, (i + 1) % count) for i in range(ends)])  291 us
    add x64, other arithmetic, sweep_body(): iterate = iterate + direction  96.8 us
    ppermute x66, starting transfers between devices, padded_2(): lax.ppermute(head, axis, [((i + 1) % count, i) for i in range(ends)])  85.3 us
    dynamic_slice x64, local copies, waits for them, and re-layouts, sweep_body(): step_table[sweep_index] * (inverse_diag * residual)  39.7 us
    dynamic_slice x64, local copies, waits for them, and re-layouts, sweep_body(): keep_table[sweep_index] * direction  38.7 us
    reduce_scatter x1, waiting for transfers between devices, shards(): lax.psum_scatter(partial_grad, 'test', scatter_dimension=0, tiled=True)  21.9 us
  transfers between devices with their start and end apart: 134, of which 4 were waited for; matrix products, arithmetic and copies ran while one was open for 12% of the time, Pallas kernels for 0%

commit v1 on v0

v1 whole, which is shorter than its diff:
```python
import functools
import math

import jax
import jax.numpy as jnp
import numpy as np
from jax import lax
from jax.experimental import pallas as pl
from jax.experimental.pallas import tpu as pltpu
from jax.sharding import PartitionSpec as P

ITERS = 32
CORR = 16
LOW = 0.1
HIGH = 2.0
PUMP_RATE = 8.0
NOISE_VAR = 0.01
NUGGET = 1.0
SMOOTH = 2.0
HIGHEST = lax.Precision.HIGHEST
UNROLL = 8


def sweep_constants():
    centre = 0.5 * (HIGH + LOW)
    span = 0.5 * (HIGH - LOW)
    ratio = centre / span
    rho = 1.0 / ratio
    own, keep, step = [], [], []
    for _ in range(ITERS):
        rho_new = 1.0 / (2.0 * ratio - rho)
        keep.append(rho_new * rho)
        step.append(2.0 * rho_new / span)
        own.append(1.0 + keep[-1] - step[-1])
        rho = rho_new
    return np.array([own, keep, step], np.float32)


def fourier_basis(length):
    where = np.arange(length)
    rows, freqs = [], []
    for freq in range(length // 2 + 1):
        angle = 2.0 * np.pi / length * ((freq * where) % length)
        edge = freq == 0 or 2 * freq == length
        scale = math.sqrt((1.0 if edge else 2.0) / length)
        rows.append(scale * np.cos(angle))
        freqs.append(freq)
        if not edge:
            rows.append(scale * np.sin(angle))
            freqs.append(freq)
    return np.stack(rows), np.array(freqs, np.float64)


def prior_table(freq_x, full_x, freq_y, full_y):
    wave_x = freq_x * (2.0 * np.pi / full_x)
    wave_y = freq_y * (2.0 * np.pi / full_y)
    wave_sq = wave_x[:, None] ** 2 + wave_y[None, :] ** 2
    return NUGGET + SMOOTH * CORR**2 / (1.0 + CORR**2 * wave_sq) ** 2


def solve_kernel(
    slab, consts, place, pump, ports, heads, cells, out,
    cond, inv, c_zm, c_zp, c_xm, c_xp, c_ym, c_yp, rhs, head_a, head_b, adj_a, adj_b,
):
    full_x = cells.shape[0]
    depth, width = cells.shape[2:]
    z_at = lax.broadcasted_iota(jnp.int32, (depth, width), 0)
    y_at = lax.broadcasted_iota(jnp.int32, (depth, width), 1)
    z_lo, z_hi = z_at == 0, z_at == depth - 1
    y_lo, y_hi = y_at == 0, y_at == width - 1
    blank = jnp.zeros((depth, width), jnp.float32)

    def z_before(v):
        return pltpu.roll(v, 1, 0)

    def z_after(v):
        return pltpu.roll(v, depth - 1, 0)

    def y_before(v):
        return pltpu.roll(v, 1, 1)

    def y_after(v):
        return pltpu.roll(v, width - 1, 1)

    for field in (cond, head_a, head_b, adj_a, adj_b):
        field[0] = blank
        field[full_x + 1] = blank

    def rows(body):
        @pl.loop(0, full_x // UNROLL)
        def _(block):
            for inner in range(UNROLL):
                body(block * UNROLL + inner)

    def fill(x):
        cond[x + 1] = jnp.exp(cells[x, 0])

    rows(fill)
    first = 1.0 / (0.5 * (HIGH + LOW))

    def faces(x):
        here = cond[x + 1]
        f_zm = 0.5 * (here + jnp.where(z_lo, 0.0, z_before(here)))
        f_zp = 0.5 * (here + jnp.where(z_hi, 0.0, z_after(here)))
        f_xm = 0.5 * (here + cond[x])
        f_xp = 0.5 * (here + cond[x + 2])
        f_ym = 0.5 * (here + jnp.where(y_lo, 0.0, y_before(here)))
        f_yp = 0.5 * (here + jnp.where(y_hi, 0.0, y_after(here)))
        scale = 1.0 / (cells[x, 1] + f_zm + f_zp + f_xm + f_xp + f_ym + f_yp)
        inv[x] = scale
        c_zm[x] = jnp.where(z_lo, 0.0, f_zm * scale)
        c_zp[x] = jnp.where(z_hi, 0.0, f_zp * scale)
        c_xm[x] = f_xm * scale
        c_xp[x] = f_xp * scale
        c_ym[x] = jnp.where(y_lo, 0.0, f_ym * scale)
        c_yp[x] = jnp.where(y_hi, 0.0, f_yp * scale)
        rhs[x] = cells[x, 2] * scale

    rows(faces)

    def split(cell):
        plane = full_x * width
        rest = lax.rem(cell, plane)
        return lax.div(cell, plane), lax.div(rest, width), lax.rem(rest, width)

    def solve(now, other):
        def start(x):
            now[x + 1] = rhs[x] * first
            other[x + 1] = blank

        rows(start)

        def sweep(src, dst, own, keep, step):
            @pl.loop(0, full_x // UNROLL)
            def _(block):
                base = block * UNROLL
                left = src[base]
                here = src[base + 1]
                for inner in range(UNROLL):
                    x = base + inner
                    right = src[x + 2]
                    total = rhs[x] + c_xm[x] * left + c_xp[x] * right
                    total += c_zm[x] * z_before(here) + c_zp[x] * z_after(here)
                    total += c_ym[x] * y_before(here) + c_yp[x] * y_after(here)
                    dst[x + 1] = own * here - keep * dst[x + 1] + step * total
                    left, here = here, right

        @pl.loop(0, ITERS // 2)
        def _(pair):
            k = 2 * pair
            sweep(now, other, consts[0, k], consts[1, k], consts[2, k])
            sweep(other, now, consts[0, k + 1], consts[1, k + 1], consts[2, k + 1])

    z, x, y = split(pump[0])
    spot = (z_at == z) & (y_at == y)
    rhs[x] = rhs[x] + jnp.where(spot, -PUMP_RATE * inv[x], 0.0)
    solve(head_a, head_b)

    def clear(x):
        rhs[x] = blank

    rows(clear)

    @pl.loop(0, ports.shape[1])
    def _(port):
        z, x, y = split(ports[0, port])
        spot = (z_at == z) & (y_at == y)
        misfit = (head_a[x + 1] - heads[0, port]) * (1.0 / NOISE_VAR)
        rhs[x] = rhs[x] + jnp.where(spot, misfit * inv[x], 0.0)

    solve(adj_a, adj_b)

    first_row = place[0]
    for row in range(slab):
        x = first_row + row
        h, a = head_a[x + 1], adj_a[x + 1]
        total = (a - adj_a[x]) * (h - head_a[x])
        total += (a - adj_a[x + 2]) * (h - head_a[x + 2])
        for move, mask in ((z_before, z_lo), (z_after, z_hi), (y_before, y_lo), (y_after, y_hi)):
            total += (a - jnp.where(mask, 0.0, move(a))) * (h - jnp.where(mask, 0.0, move(h)))
        out[row] = -0.5 * cond[x + 1] * total


def shards(log_conductivity, storage, recharge, pump_cells, obs_cells, obs_heads):
    depth, slab, width = log_conductivity.shape
    dom_count = lax.axis_size("dom")
    dom_index = lax.axis_index("dom")
    full_x = slab * dom_count
    fields = jnp.stack([log_conductivity, storage, recharge]).transpose(2, 0, 1, 3)
    cells = lax.all_gather(fields, "dom", axis=0, tiled=True)
    whole = pltpu.VMEM((full_x, depth, width), jnp.float32)
    padded = pltpu.VMEM((full_x + 2, depth, width), jnp.float32)
    smem = pl.BlockSpec(memory_space=pltpu.SMEM)
    vmem = pl.BlockSpec(memory_space=pltpu.VMEM)
    partial = pl.pallas_call(
        functools.partial(solve_kernel, slab),
        out_shape=jax.ShapeDtypeStruct((slab, depth, width), jnp.float32),
        in_specs=[smem] * 5 + [vmem],
        out_specs=vmem,
        scratch_shapes=[padded] + [whole] * 8 + [padded] * 4,
        compiler_params=pltpu.CompilerParams(vmem_limit_bytes=56 * 1024 * 1024),
    )(
        jnp.asarray(sweep_constants()),
        (dom_index * slab).astype(jnp.int32).reshape(1),
        pump_cells,
        obs_cells,
        obs_heads,
        cells,
    )
    gradient = lax.psum_scatter(
        partial.transpose(1, 0, 2), "test", scatter_dimension=0, tiled=True
    )
    layers = gradient.shape[0]
    basis_x, freq_x = fourier_basis(full_x)
    basis_y, freq_y = fourier_basis(width)
    weights = jnp.asarray(prior_table(freq_x, full_x, freq_y, width), jnp.float32)
    basis_x = jnp.asarray(basis_x, jnp.float32)
    basis_y = jnp.asarray(basis_y, jnp.float32)
    spectral = jnp.dot(gradient.reshape(-1, width), basis_y.T, precision=HIGHEST)
    spectral = lax.all_gather(
        spectral.reshape(layers, slab, width), "dom", axis=1, tiled=True
    )
    filtered = jnp.einsum("fx,mxk->mfk", basis_x, spectral, precision=HIGHEST) * weights
    own_x = lax.dynamic_slice_in_dim(basis_x, dom_index * slab, slab, axis=1)
    back = jnp.einsum("fx,mfk->mxk", own_x, filtered, precision=HIGHEST)
    step_field = jnp.dot(back.reshape(-1, width), basis_y, precision=HIGHEST)
    return gradient, step_field.reshape(layers, slab, width)


def solution(mesh):
    in_specs = (
        P("grp", "dom", None),
        P("grp", "dom", None),
        P("grp", "dom", None),
        P(("grp", "test")),
        P(("grp", "test"), None),
        P(("grp", "test"), None),
    )
    out_specs = (P(("grp", "test"), "dom", None), P(("grp", "test"), "dom", None))
    return jax.shard_map(shards, mesh=mesh, in_specs=in_specs, out_specs=out_specs, check_vma=False)
```

time: 658 us -> 111 us (0.17)
  starting transfers between devices: 380 us -> 0.08 us
  other arithmetic: 105 us -> 0.78 us
  local copies, waits for them, and re-layouts: 90.5 us -> 3.78 us
  Pallas kernels: 0 us -> 40.1 us
  matrix products: 21.9 us -> 4.58 us
  waiting for transfers between devices: 29.8 us -> 41.2 us
    ppermute x132 -> x0, starting transfers between devices: 377 us -> none  [the longest x66 291 us: padded_2(): lax.ppermute(tail, axis, [(i, (i + 1) % count) for i in range(ends)])]
    add x65 -> x0, other arithmetic: 96.9 us -> none  [the longest x64 96.8 us: sweep_body(): iterate = iterate + direction]
    dynamic_slice x128 -> x0, local copies, waits for them, and re-layouts: 78.4 us -> none  [the longest x64 39.7 us: sweep_body(): step_table[sweep_index] * (inverse_diag * residual)]
    pallas_call x0 -> x1, Pallas kernels: none -> 40.1 us  [shards(): pl.pallas_call(functools.partial(solve_kernel, slab), out_shape=jax.Shape...]
    all_gather x0 -> x1, waiting for transfers between devices: none -> 21.8 us  [shards(): cells = lax.all_gather(fields, 'dom', axis=0, tiled=True)]
    dot_general x12 -> x4, matrix products: 21.9 us -> 4.58 us  [the longest x1 1.72 us: shards(): jnp.dot(gradient.reshape(-1, width), basis_y.T, precision=HIGHEST)]
  transfers between devices with their start and end apart: 134 -> 2, of which waited for: 4 -> 2; matrix products, arithmetic and copies ran while one was open for 12% -> 0% of each run, Pallas kernels for 0% -> 0%
where the time goes in v1:
time: 111 us
  waiting for transfers between devices  41.2 us (37%)
  Pallas kernels  40.1 us (36%)
  between operations  14.7 us (13%)
  blocking collectives  5.43 us (5%)
  matrix products  4.58 us (4%)
  local copies, waits for them, and re-layouts  3.78 us (3%)
    pallas_call x1, Pallas kernels, shards(): pl.pallas_call(functools.partial(solve_kernel, slab), out_shape=jax.Shape...  40.1 us
    all_gather x1, waiting for transfers between devices, shards(): cells = lax.all_gather(fields, 'dom', axis=0, tiled=True)  21.8 us
    reduce_scatter x1, waiting for transfers between devices, shards(): lax.psum_scatter(partial.transpose(1, 0, 2), 'test', scatter_dimension=0,...  19.3 us
    all_gather x1, blocking collectives, shards(): lax.all_gather(spectral.reshape(layers, slab, width), 'dom', axis=1, tile...  5.43 us
  transfers between devices with their start and end apart: 2, of which 2 were waited for; matrix products, arithmetic and copies ran while one was open for 0% of the time, Pallas kernels for 0%

profile of v1, /device:TPU:0, one launch (start us, length us, event | category | flops | bytes accessed | tf_op | source)
XLA Modules:
  0.0 110.7 jit_solution(11841806940048067664)
XLA Ops:
  7.2 0.0 all-gather.2.cloned.1.call-start
  7.2 1.0 copy.23
  8.2 1.1 %copy_bitcast_fusion = (f32[1,8,8,512]{3,1,0,2:T(8,128)S(1)}, f32[1,8,8,512]{3,1,0,2:T(8,128)S(1)}) fusion(f32[8,8,512]{2,1,0:T(8,128)} %param.12, f32[8,8,512]{2,1,0:T(8,128)} %param.11), kind=kLoop, calls=%fused_computation.4 | loop fusion | bytes 524288 | tf_op jit(solution)/shard_map/stack | solution.py:189
  9.3 0.0 copy-start
  9.3 0.8 maximum_bitcast_fusion
  10.1 0.0 all-gather.2.cloned.1.call-update
  10.1 0.0 reduce-scatter.2.cloned.1.call-start
  10.8 21.8 %all-gather.2.cloned.1.call-done.cells = f32[32,3,8,512]{3,2,1,0:T(8,128)} async-done(((f32[8,3,8,512]{3,2,1,0:T(8,128)}), f32[32,3,8,512]{3,2,1,0:T(8,128)}) %all-gather.2.cloned.1.call-update) | async-done | bytes 1572880 | tf_op jit(solution)/shard_map/all_gather | solution.py:190
  32.7 0.0 copy-start.1
  32.7 0.0 copy-start.2
  32.7 40.1 %shard_map.113 = f32[8,8,512]{2,1,0:T(8,128)} custom-call(f32[3,32]{1,0:T(4,128)} %constant.19.clone.consts, s32[1]{0:T(128)} %bitcast.place, s32[1]{0:T(128)S(6)} %copy.24.pump, s32[1,32]{1,0:T(1,128)} %ports.1, f32[1,32]{1,0:T(1,128)} %heads.1, f32[32,3,8,512]{3,2,1,0:T(8,128)} %all-gather.2.cloned.1.call-done.cells), custom_call_target="tpu_custom_call" | custom-call | tf_op jit(solution)/shard_map/pallas_call | solution.py:195
  72.8 0.0 copy-start.3
  72.8 1.6 %copy.19 = f32[8,8,512]{2,1,0:T(8,128)} copy(f32[8,8,512]{2,0,1:T(8,128)} %bitcast.30) | data formatting | bytes 262144 | tf_op jit(solution)/shard_map/transpose | solution.py:211
  74.5 0.0 reduce-scatter.2.cloned.1.call-update
  74.5 19.3 %reduce-scatter.2.cloned.1.call-done = f32[2,8,512]{2,1,0:T(8,128)} async-done(((f32[8,8,512]{2,1,0:T(8,128)}), f32[2,8,512]{2,1,0:T(8,128)}) %reduce-scatter.2.cloned.1.call-update) | async-done | bytes 32784 | tf_op jit(solution)/shard_map/reduce_scatter | solution.py:210
  93.8 0.0 copy-done
  93.8 1.7 %fusion.4 = f32[2,8,512]{2,1,0:T(8,128)S(1)} fusion(f32[2,8,512]{2,1,0:T(8,128)} %reduce-scatter.2.cloned.1.call-done, f32[512,512,1]{1,0,2:T(8,128)S(1)} %copy-done), kind=kOutput, calls=%fused_computation.10 | convolution fusion | flops 50331648 | bytes 1114112 | tf_op jit(solution)/shard_map/dot_general | solution.py:219
  95.5 5.4 %all_gather.7 = f32[2,32,512]{2,1,0:T(8,128)S(1)} all-gather(f32[2,8,512]{2,1,0:T(8,128)S(1)} %fusion.4), channel_id=1, replica_groups=mesh['grp'=2,'dom'=4,'test'=4] {'dom'}, dimensions={1}, use_global_device_ids=true | all-gather | bytes 163840 | tf_op jit(solution)/shard_map/all_gather | solution.py:220
  101.0 0.0 copy-done.1
  101.0 0.0 copy-done.2
  101.0 1.0 fusion
  102.0 0.0 copy-done.3
  102.0 0.6 convolution_bitcast_fusion.1
  102.6 1.3 %fusion.5 = f32[2,8,512]{2,1,0:T(8,128)} fusion(f32[2,8,512]{2,1,0:T(8,128)S(1)} %convolution_bitcast_fusion.1, f32[512,512,1]{1,0,2:T(8,128)S(1)} %copy-done), kind=kOutput, calls=%fused_computation.11 | convolution fusion | flops 50331648 | bytes 1114112 | tf_op jit(solution)/shard_map/dot_general | solution.py:226
Async XLA Ops:
  7.2 25.5 %all-gather.2.cloned.1.call-start = ((), (), s32[]{:S(2)}) async-start(), calls=%async_computation.1 | async-start | bytes 1966080 | tf_op jit(solution)/shard_map/all_gather | solution.py:190
  9.3 84.5 %copy-start = (f32[512,512,1]{1,0,2:T(8,128)S(1)}, f32[512,512,1]{1,0,2:T(8,128)}, u32[]{:S(2)}) copy-start(f32[512,512,1]{1,0,2:T(8,128)} %constant.26) | copy-start | bytes 3145732
  10.1 83.7 %reduce-scatter.2.cloned.1.call-start = ((), (), s32[]{:S(2)}) async-start(), calls=%async_computation.2 | async-start | bytes 163840 | tf_op jit(solution)/shard_map/reduce_scatter | solution.py:210
  32.7 68.3 %copy-start.1 = (f32[32,512]{0,1:T(8,128)S(1)}, f32[32,512]{0,1:T(8,128)}, u32[]{:S(2)}) copy-start(f32[32,512]{0,1:T(8,128)} %constant.20.clone) | copy-start | bytes 196612
  32.7 68.3 %copy-start.2 = (f32[32,32,1]{1,0,2:T(8,128)S(1)}, f32[32,32,1]{1,0,2:T(8,128)}, u32[]{:S(2)}) copy-start(f32[32,32,1]{1,0,2:T(8,128)} %constant.27) | copy-start | bytes 12292
  72.8 29.2 %copy-start.3 = (f32[32,32]{1,0:T(8,128)S(1)}, f32[32,32]{1,0:T(8,128)}, u32[]{:S(2)}) copy-start(f32[32,32]{1,0:T(8,128)} %constant.21.clone) | copy-start | bytes 12292
Sparse Core Ops, SparseCore 0:
  10.3 22.3 all-gather.1
  74.6 19.1 reduce-scatter.1

commit v2 on v1

--- a/solution.py
+++ b/solution.py
@@ -19,6 +19,8 @@
 SMOOTH = 2.0
 HIGHEST = lax.Precision.HIGHEST
 UNROLL = 8
+MESH = pl.DeviceIdType.MESH
+VMEM_LIMIT = 56 * 1024 * 1024
 
 
 def sweep_constants():
@@ -58,11 +60,130 @@
     return NUGGET + SMOOTH * CORR**2 / (1.0 + CORR**2 * wave_sq) ** 2
 
 
+def gather_kernel(
+    count, conduct, storage, recharge, cells, near_send, near_recv, far_send, far_recv
+):
+    slab = conduct.shape[1]
+    chips = count // 2
+    me = lax.axis_index("dom")
+    core, chip = lax.rem(me, 2), lax.div(me, 2)
+    twin = me + 1 - 2 * core
+    barrier = pltpu.get_barrier_semaphore()
+
+    def far(hop):
+        return 2 * lax.rem(chip + hop, chips) + core
+
+    for peer in [twin] + [far(hop) for hop in range(1, chips)]:
+        pl.semaphore_signal(barrier, 1, device_id={"dom": peer}, device_id_type=MESH)
+
+    def block(field, owner):
+        return cells.at[field, pl.ds(owner * slab, slab)]
+
+    def near_copy(slot, field, owner):
+        return pltpu.make_async_remote_copy(
+            src_ref=block(field, owner),
+            dst_ref=block(field, owner),
+            send_sem=near_send.at[slot, field],
+            recv_sem=near_recv.at[slot, field],
+            device_id={"dom": twin},
+            device_id_type=MESH,
+        )
+
+    def far_copy(hop, field, owner):
+        return pltpu.make_async_remote_copy(
+            src_ref=block(field, owner),
+            dst_ref=block(field, owner),
+            send_sem=far_send.at[hop - 1, field],
+            recv_sem=far_recv.at[hop - 1, field],
+            device_id={"dom": far(hop)},
+            device_id_type=MESH,
+        )
+
+    own = pl.ds(me * slab, slab)
+    for field, ref in enumerate((conduct, storage, recharge)):
+        values = jnp.swapaxes(ref[...], 0, 1)
+        cells[field, own] = jnp.exp(values) if field == 0 else values
+        if field == 0:
+            pl.semaphore_wait(barrier, chips)
+        for hop in range(1, chips):
+            far_copy(hop, field, me).start()
+        near_copy(0, field, me).start()
+    for hop in range(1, chips):
+        source = far(chips - hop)
+        for field in range(3):
+            far_copy(hop, field, source).wait_recv()
+            near_copy(hop, field, source).start()
+    for field in range(3):
+        for hop in range(1, chips):
+            far_copy(hop, field, me).wait_send()
+        for hop in range(chips):
+            mine = me if hop == 0 else far(chips - hop)
+            near_copy(hop, field, mine).wait_send()
+            near_copy(hop, field, mine + 1 - 2 * core).wait_recv()
+
+
+def reduce_kernel(
+    tests, count, part, grad, full, landing, test_send, test_recv, dom_send, dom_recv
+):
+    layers, slab = grad.shape[:2]
+    test, me = lax.axis_index("test"), lax.axis_index("dom")
+    barrier = pltpu.get_barrier_semaphore()
+
+    def test_at(hop):
+        return lax.rem(test + hop, tests)
+
+    def dom_at(hop):
+        return lax.rem(me + hop, count)
+
+    for hop in range(1, tests):
+        pl.semaphore_signal(barrier, 1, device_id={"test": test_at(hop)}, device_id_type=MESH)
+    for hop in range(1, count):
+        pl.semaphore_signal(barrier, 1, device_id={"dom": dom_at(hop)}, device_id_type=MESH)
+    pl.semaphore_wait(barrier, tests + count - 2)
+
+    def test_copy(hop):
+        return pltpu.make_async_remote_copy(
+            src_ref=part.at[pl.ds(test_at(hop) * layers, layers)],
+            dst_ref=landing.at[hop - 1],
+            send_sem=test_send.at[hop - 1],
+            recv_sem=test_recv.at[hop - 1],
+            device_id={"test": test_at(hop)},
+            device_id_type=MESH,
+        )
+
+    def dom_copy(hop, owner):
+        place = full.at[:, pl.ds(owner * slab, slab)]
+        return pltpu.make_async_remote_copy(
+            src_ref=place,
+            dst_ref=place,
+            send_sem=dom_send.at[hop - 1],
+            recv_sem=dom_recv.at[hop - 1],
+            device_id={"dom": dom_at(hop)},
+            device_id_type=MESH,
+        )
+
+    for hop in range(1, tests):
+        test_copy(hop).start()
+    total = part[pl.ds(test * layers, layers)]
+    for hop in range(1, tests):
+        test_copy(hop).wait_recv()
+        total = total + landing[hop - 1]
+    grad[...] = total
+    full[:, pl.ds(me * slab, slab)] = total
+    for hop in range(1, count):
+        dom_copy(hop, me).start()
+    for hop in range(1, tests):
+        test_copy(hop).wait_send()
+    for hop in range(1, count):
+        dom_copy(hop, me).wait_send()
+        dom_copy(hop, dom_at(count - hop)).wait_recv()
+
+
 def solve_kernel(
     slab, consts, place, pump, ports, heads, cells, out,
-    cond, inv, c_zm, c_zp, c_xm, c_xp, c_ym, c_yp, rhs, head_a, head_b, adj_a, adj_b,
+    cond, inv, c_zm, c_zp, c_xm, c_xp, c_ym, c_yp, rhs, head_a, head_b, adj_a, adj_b, terms,
 ):
-    full_x = cells.shape[0]
+    full_x = cells.shape[1]
     depth, width = cells.shape[2:]
     z_at = lax.broadcasted_iota(jnp.int32, (depth, width), 0)
     y_at = lax.broadcasted_iota(jnp.int32, (depth, width), 1)
@@ -93,7 +214,7 @@
                 body(block * UNROLL + inner)
 
     def fill(x):
-        cond[x + 1] = jnp.exp(cells[x, 0])
+        cond[x + 1] = cells[0, x]
 
     rows(fill)
     first = 1.0 / (0.5 * (HIGH + LOW))
@@ -106,7 +227,7 @@
         f_xp = 0.5 * (here + cond[x + 2])
         f_ym = 0.5 * (here + jnp.where(y_lo, 0.0, y_before(here)))
         f_yp = 0.5 * (here + jnp.where(y_hi, 0.0, y_after(here)))
-        scale = 1.0 / (cells[x, 1] + f_zm + f_zp + f_xm + f_xp + f_ym + f_yp)
+        scale = 1.0 / (cells[1, x] + f_zm + f_zp + f_xm + f_xp + f_ym + f_yp)
         inv[x] = scale
         c_zm[x] = jnp.where(z_lo, 0.0, f_zm * scale)
         c_zp[x] = jnp.where(z_hi, 0.0, f_zp * scale)
@@ -114,7 +235,7 @@
         c_xp[x] = f_xp * scale
         c_ym[x] = jnp.where(y_lo, 0.0, f_ym * scale)
         c_yp[x] = jnp.where(y_hi, 0.0, f_yp * scale)
-        rhs[x] = cells[x, 2] * scale
+        rhs[x] = cells[2, x] * scale
 
     rows(faces)
 
@@ -178,7 +299,8 @@
         total += (a - adj_a[x + 2]) * (h - head_a[x + 2])
         for move, mask in ((z_before, z_lo), (z_after, z_hi), (y_before, y_lo), (y_after, y_hi)):
             total += (a - jnp.where(mask, 0.0, move(a))) * (h - jnp.where(mask, 0.0, move(h)))
-        out[row] = -0.5 * cond[x + 1] * total
+        terms[row] = -0.5 * cond[x + 1] * total
+    out[...] = jnp.swapaxes(terms[...], 0, 1)
 
 
 def shards(log_conductivity, storage, recharge, pump_cells, obs_cells, obs_heads):
@@ -186,19 +308,30 @@
     dom_count = lax.axis_size("dom")
     dom_index = lax.axis_index("dom")
     full_x = slab * dom_count
-    fields = jnp.stack([log_conductivity, storage, recharge]).transpose(2, 0, 1, 3)
-    cells = lax.all_gather(fields, "dom", axis=0, tiled=True)
     whole = pltpu.VMEM((full_x, depth, width), jnp.float32)
     padded = pltpu.VMEM((full_x + 2, depth, width), jnp.float32)
     smem = pl.BlockSpec(memory_space=pltpu.SMEM)
     vmem = pl.BlockSpec(memory_space=pltpu.VMEM)
+    chips = dom_count // 2
+    cells = pl.pallas_call(
+        functools.partial(gather_kernel, dom_count),
+        out_shape=jax.ShapeDtypeStruct((3, full_x, depth, width), jnp.float32),
+        in_specs=[vmem] * 3,
+        out_specs=vmem,
+        scratch_shapes=[pltpu.SemaphoreType.DMA((chips, 3))] * 2
+        + [pltpu.SemaphoreType.DMA((max(chips - 1, 1), 3))] * 2,
+        compiler_params=pltpu.CompilerParams(
+            collective_id=0, has_side_effects=True, vmem_limit_bytes=VMEM_LIMIT
+        ),
+    )(log_conductivity, storage, recharge)
     partial = pl.pallas_call(
         functools.partial(solve_kernel, slab),
-        out_shape=jax.ShapeDtypeStruct((slab, depth, width), jnp.float32),
+        out_shape=jax.ShapeDtypeStruct((depth, slab, width), jnp.float32),
         in_specs=[smem] * 5 + [vmem],
         out_specs=vmem,
-        scratch_shapes=[padded] + [whole] * 8 + [padded] * 4,
-        compiler_params=pltpu.CompilerParams(vmem_limit_bytes=56 * 1024 * 1024),
+        scratch_shapes=[padded] + [whole] * 8 + [padded] * 4
+        + [pltpu.VMEM((slab, depth, width), jnp.float32)],
+        compiler_params=pltpu.CompilerParams(vmem_limit_bytes=VMEM_LIMIT),
     )(
         jnp.asarray(sweep_constants()),
         (dom_index * slab).astype(jnp.int32).reshape(1),
@@ -207,19 +340,30 @@
         obs_heads,
         cells,
     )
-    gradient = lax.psum_scatter(
-        partial.transpose(1, 0, 2), "test", scatter_dimension=0, tiled=True
-    )
-    layers = gradient.shape[0]
+    tests = lax.axis_size("test")
+    layers = depth // tests
+    gradient, full = pl.pallas_call(
+        functools.partial(reduce_kernel, tests, dom_count),
+        out_shape=(
+            jax.ShapeDtypeStruct((layers, slab, width), jnp.float32),
+            jax.ShapeDtypeStruct((layers, full_x, width), jnp.float32),
+        ),
+        in_specs=[vmem],
+        out_specs=(vmem, vmem),
+        scratch_shapes=[pltpu.VMEM((tests - 1, layers, slab, width), jnp.float32)]
+        + [pltpu.SemaphoreType.DMA((tests - 1,))] * 2
+        + [pltpu.SemaphoreType.DMA((dom_count - 1,))] * 2,
+        compiler_params=pltpu.CompilerParams(
+            collective_id=1, has_side_effects=True, vmem_limit_bytes=VMEM_LIMIT
+        ),
+    )(partial)
     basis_x, freq_x = fourier_basis(full_x)
     basis_y, freq_y = fourier_basis(width)
     weights = jnp.asarray(prior_table(freq_x, full_x, freq_y, width), jnp.float32)
     basis_x = jnp.asarray(basis_x, jnp.float32)
     basis_y = jnp.asarray(basis_y, jnp.float32)
-    spectral = jnp.dot(gradient.reshape(-1, width), basis_y.T, precision=HIGHEST)
-    spectral = lax.all_gather(
-        spectral.reshape(layers, slab, width), "dom", axis=1, tiled=True
-    )
+    spectral = jnp.dot(full.reshape(-1, width), basis_y.T, precision=HIGHEST)
+    spectral = spectral.reshape(layers, full_x, width)
     filtered = jnp.einsum("fx,mxk->mfk", basis_x, spectral, precision=HIGHEST) * weights
     own_x = lax.dynamic_slice_in_dim(basis_x, dom_index * slab, slab, axis=1)
     back = jnp.einsum("fx,mfk->mxk", own_x, filtered, precision=HIGHEST)

time: 111 us -> 75.6 us (0.68)
  waiting for transfers between devices: 41.2 us -> 0 us
  Pallas kernels: 40.1 us -> 68.5 us
  between operations: 14.7 us -> 1.37 us
  blocking collectives: 5.43 us -> 0 us
  local copies, waits for them, and re-layouts: 3.78 us -> 0.64 us
    pallas_call x0 -> x2, Pallas kernels: none -> 28.4 us  [the longest x1 16.2 us: shards(): pl.pallas_call(functools.partial(gather_kernel, dom_count), out_shape=jax...]
    all_gather x1 -> x0, waiting for transfers between devices: 21.8 us -> none  [shards(): cells = lax.all_gather(fields, 'dom', axis=0, tiled=True)]
    reduce_scatter x1 -> x0, waiting for transfers between devices: 19.3 us -> none  [shards(): lax.psum_scatter(partial.transpose(1, 0, 2), 'test', scatter_dimension=0,...]
    all_gather x1 -> x0, blocking collectives: 5.43 us -> none  [shards(): lax.all_gather(spectral.reshape(layers, slab, width), 'dom', axis=1, tile...]
    transpose x1 -> x0, local copies, waits for them, and re-layouts: 1.65 us -> none  [shards(): partial.transpose(1, 0, 2)]
    another operation x1 -> x0, local copies, waits for them, and re-layouts: 1.13 us -> none  [shards(): jnp.stack([log_conductivity, storage, recharge]).transpose(2, 0, 1, 3)]
  transfers between devices with their start and end apart: 2 -> 0, of which waited for: 2 -> 0; matrix products, arithmetic and copies ran while one was open for 0% -> 0% of each run, Pallas kernels for 0% -> 0%
where the time goes in v2:
time: 75.6 us; the launch traced here: 75.4 us
  Pallas kernels  68.5 us (91%)
  matrix products  4.88 us (6%)
  between operations  1.37 us (2%)
    pallas_call x1, Pallas kernels, shards(): pl.pallas_call(functools.partial(solve_kernel, slab), out_shape=jax.Shape...  40.1 us
    pallas_call x1, Pallas kernels, shards(): pl.pallas_call(functools.partial(gather_kernel, dom_count), out_shape=jax...  16.2 us
    pallas_call x1, Pallas kernels, shards(): pl.pallas_call(functools.partial(reduce_kernel, tests, dom_count), out_sh...  12.2 us
    dot_general x1, matrix products, shards(): spectral = jnp.dot(full.reshape(-1, width), basis_y.T, precision=HIGHEST)  2.02 us

profile of v2, /device:TPU:0, one launch (start us, length us, event | category | flops | bytes accessed | tf_op | source)
XLA Modules:
  0.0 75.4 jit_solution(14978751435257728298)
XLA Ops:
  1.3 0.0 copy-start
  1.3 16.2 %shard_map.113.cells = f32[3,32,8,512]{3,2,1,0:T(8,128)} custom-call(f32[8,8,512]{2,1,0:T(8,128)} %conduct.1, f32[8,8,512]{2,1,0:T(8,128)} %storage.1, f32[8,8,512]{2,1,0:T(8,128)} %recharge.1), custom_call_target="tpu_custom_call" | custom-call | tf_op jit(solution)/shard_map/pallas_call | solution.py:316
  17.5 0.0 copy-start.1
  17.5 0.0 copy-start.3
  17.5 40.1 %shard_map.114.part = f32[8,8,512]{2,1,0:T(8,128)} custom-call(f32[3,32]{1,0:T(4,128)} %constant.19.clone.consts, s32[1]{0:T(128)} %bitcast.place, s32[1]{0:T(128)S(6)} %copy.13.pump, s32[1,32]{1,0:T(1,128)} %ports.1, f32[1,32]{1,0:T(1,128)} %heads.1, f32[3,32,8,512]{3,2,1,0:T(8,128)} %shard_map.113.cells), custom_call_target="tpu_custom_call" | custom-call | tf_op jit(solution)/shard_map/pallas_call | solution.py:327
  57.6 0.0 copy-start.4
  57.6 12.2 %shard_map.115 = (f32[2,8,512]{2,1,0:T(8,128)}, f32[2,32,512]{2,1,0:T(8,128)}) custom-call(f32[8,8,512]{2,1,0:T(8,128)} %shard_map.114.part), custom_call_target="tpu_custom_call" | custom-call | tf_op jit(solution)/shard_map/pallas_call | solution.py:345
  69.8 0.0 copy-done
  69.8 2.0 %fusion.4 = f32[2,32,512]{2,1,0:T(8,128)S(1)} fusion(f32[2,32,512]{2,1,0:T(8,128)} %get-tuple-element.5, f32[512,512,1]{1,0,2:T(8,128)S(1)} %copy-done), kind=kOutput, calls=%fused_computation.6 | convolution fusion | flops 201326592 | bytes 1310720 | tf_op jit(solution)/shard_map/dot_general | solution.py:365
  71.9 0.0 copy-done.1
  71.9 0.0 copy-done.3
  71.9 0.0 copy-start.2
  71.9 1.0 %fusion = f32[2,32,512]{1,2,0:T(8,128)S(1)} fusion(f32[2,32,512]{2,1,0:T(8,128)S(1)} %fusion.4, f32[32,32,1]{1,0,2:T(8,128)S(1)} %copy-done.3, f32[32,512]{0,1:T(8,128)S(1)} %copy-done.1), kind=kOutput, calls=%fused_computation.1 | convolution fusion | flops 12615680 | bytes 331776 | tf_op jit(solution)/shard_map/fx,mxk->mfk/dot_general | solution.py:367
  72.9 0.0 copy-done.4
  72.9 0.6 convolution_bitcast_fusion.1
  73.5 1.3 %fusion.5 = f32[2,8,512]{2,1,0:T(8,128)} fusion(f32[2,8,512]{2,1,0:T(8,128)S(1)} %convolution_bitcast_fusion.1, f32[512,512,1]{1,0,2:T(8,128)S(1)} %copy-done), kind=kOutput, calls=%fused_computation.7 | convolution fusion | flops 50331648 | bytes 1114112 | tf_op jit(solution)/shard_map/dot_general | solution.py:370
  74.8 0.0 copy-done.2
  74.8 0.6 copy.14
Async XLA Ops:
  1.3 68.6 %copy-start = (f32[512,512,1]{1,0,2:T(8,128)S(1)}, f32[512,512,1]{1,0,2:T(8,128)}, u32[]{:S(2)}) copy-start(f32[512,512,1]{1,0,2:T(8,128)} %constant.26) | copy-start | bytes 3145732
  17.5 54.4 %copy-start.1 = (f32[32,512]{0,1:T(8,128)S(1)}, f32[32,512]{0,1:T(8,128)}, u32[]{:S(2)}) copy-start(f32[32,512]{0,1:T(8,128)} %constant.20.clone) | copy-start | bytes 196612
  17.5 54.4 %copy-start.3 = (f32[32,32,1]{1,0,2:T(8,128)S(1)}, f32[32,32,1]{1,0,2:T(8,128)}, u32[]{:S(2)}) copy-start(f32[32,32,1]{1,0,2:T(8,128)} %constant.27) | copy-start | bytes 12292
  57.6 15.3 %copy-start.4 = (f32[32,32]{1,0:T(8,128)S(1)}, f32[32,32]{1,0:T(8,128)}, u32[]{:S(2)}) copy-start(f32[32,32]{1,0:T(8,128)} %constant.21.clone) | copy-start | bytes 12292
  71.9 2.9 %copy-start.2 = (f32[2,8,512]{2,1,0:T(8,128)S(1)}, f32[2,8,512]{2,1,0:T(8,128)}, u32[]{:S(2)}) copy-start(f32[2,8,512]{2,1,0:T(8,128)} %get-tuple-element.8) | copy-start | bytes 98308

commit v3 on v2

--- a/solution.py
+++ b/solution.py
@@ -18,7 +18,8 @@
 NUGGET = 1.0
 SMOOTH = 2.0
 HIGHEST = lax.Precision.HIGHEST
-UNROLL = 8
+SUBLANES = 8
+LANES = 128
 MESH = pl.DeviceIdType.MESH
 VMEM_LIMIT = 56 * 1024 * 1024
 
@@ -77,7 +78,7 @@
         pl.semaphore_signal(barrier, 1, device_id={"dom": peer}, device_id_type=MESH)
 
     def block(field, owner):
-        return cells.at[field, pl.ds(owner * slab, slab)]
+        return cells.at[field, :, pl.ds(owner * slab, slab)]
 
     def near_copy(slot, field, owner):
         return pltpu.make_async_remote_copy(
@@ -102,7 +103,9 @@
     own = pl.ds(me * slab, slab)
     for field, ref in enumerate((conduct, storage, recharge)):
         values = jnp.swapaxes(ref[...], 0, 1)
-        cells[field, own] = jnp.exp(values) if field == 0 else values
+        values = jnp.exp(values) if field == 0 else values
+        for lane in range(cells.shape[1]):
+            cells[field, lane, own] = values[:, :, lane * LANES : (lane + 1) * LANES]
         if field == 0:
             pl.semaphore_wait(barrier, chips)
         for hop in range(1, chips):
@@ -183,19 +186,20 @@
     slab, consts, place, pump, ports, heads, cells, out,
     cond, inv, c_zm, c_zp, c_xm, c_xp, c_ym, c_yp, rhs, head_a, head_b, adj_a, adj_b, terms,
 ):
-    full_x = cells.shape[1]
-    depth, width = cells.shape[2:]
-    z_at = lax.broadcasted_iota(jnp.int32, (depth, width), 0)
-    y_at = lax.broadcasted_iota(jnp.int32, (depth, width), 1)
-    z_lo, z_hi = z_at == 0, z_at == depth - 1
+    depth = out.shape[0]
+    width = out.shape[2]
+    full_x = cells.shape[2] // depth
+    tiles = full_x // SUBLANES
+    s_at = lax.broadcasted_iota(jnp.int32, (SUBLANES, width), 0)
+    y_at = lax.broadcasted_iota(jnp.int32, (SUBLANES, width), 1)
     y_lo, y_hi = y_at == 0, y_at == width - 1
-    blank = jnp.zeros((depth, width), jnp.float32)
-
-    def z_before(v):
+    blank = jnp.zeros((SUBLANES, width), jnp.float32)
+
+    def s_before(v):
         return pltpu.roll(v, 1, 0)
 
-    def z_after(v):
-        return pltpu.roll(v, depth - 1, 0)
+    def s_after(v):
+        return pltpu.roll(v, SUBLANES - 1, 0)
 
     def y_before(v):
         return pltpu.roll(v, 1, 1)
@@ -203,68 +207,86 @@
     def y_after(v):
         return pltpu.roll(v, width - 1, 1)
 
-    for field in (cond, head_a, head_b, adj_a, adj_b):
-        field[0] = blank
-        field[full_x + 1] = blank
-
     def rows(body):
-        @pl.loop(0, full_x // UNROLL)
-        def _(block):
-            for inner in range(UNROLL):
-                body(block * UNROLL + inner)
-
-    def fill(x):
-        cond[x + 1] = cells[0, x]
+        @pl.loop(0, tiles)
+        def _(t):
+            for z in range(depth):
+                body(t, z)
+
+    def wrap(field):
+        for z in range(depth):
+            field[0, z] = s_before(field[tiles, z])
+            field[tiles + 1, z] = s_after(field[1, z])
+
+    def ends(t):
+        x_at = s_at * tiles + t
+        return x_at == 0, x_at == full_x - 1
+
+    def strided(field, t, z):
+        at = pl.ds(t * depth + z, SUBLANES, stride=tiles * depth)
+        return jnp.concatenate(
+            [cells[field, lane, at] for lane in range(width // LANES)], axis=1
+        )
+
+    def fill(t, z):
+        cond[t + 1, z] = strided(0, t, z)
 
     rows(fill)
+    wrap(cond)
     first = 1.0 / (0.5 * (HIGH + LOW))
 
-    def faces(x):
-        here = cond[x + 1]
-        f_zm = 0.5 * (here + jnp.where(z_lo, 0.0, z_before(here)))
-        f_zp = 0.5 * (here + jnp.where(z_hi, 0.0, z_after(here)))
-        f_xm = 0.5 * (here + cond[x])
-        f_xp = 0.5 * (here + cond[x + 2])
+    def faces(t, z):
+        x_lo, x_hi = ends(t)
+        here = cond[t + 1, z]
+        f_zm = 0.5 * (here + cond[t + 1, z - 1]) if z > 0 else 0.5 * here
+        f_zp = 0.5 * (here + cond[t + 1, z + 1]) if z < depth - 1 else 0.5 * here
+        f_xm = 0.5 * (here + jnp.where(x_lo, 0.0, cond[t, z]))
+        f_xp = 0.5 * (here + jnp.where(x_hi, 0.0, cond[t + 2, z]))
         f_ym = 0.5 * (here + jnp.where(y_lo, 0.0, y_before(here)))
         f_yp = 0.5 * (here + jnp.where(y_hi, 0.0, y_after(here)))
-        scale = 1.0 / (cells[1, x] + f_zm + f_zp + f_xm + f_xp + f_ym + f_yp)
-        inv[x] = scale
-        c_zm[x] = jnp.where(z_lo, 0.0, f_zm * scale)
-        c_zp[x] = jnp.where(z_hi, 0.0, f_zp * scale)
-        c_xm[x] = f_xm * scale
-        c_xp[x] = f_xp * scale
-        c_ym[x] = jnp.where(y_lo, 0.0, f_ym * scale)
-        c_yp[x] = jnp.where(y_hi, 0.0, f_yp * scale)
-        rhs[x] = cells[2, x] * scale
+        scale = 1.0 / (strided(1, t, z) + f_zm + f_zp + f_xm + f_xp + f_ym + f_yp)
+        inv[t, z] = scale
+        c_zm[t, z] = f_zm * scale
+        c_zp[t, z] = f_zp * scale
+        c_xm[t, z] = jnp.where(x_lo, 0.0, f_xm * scale)
+        c_xp[t, z] = jnp.where(x_hi, 0.0, f_xp * scale)
+        c_ym[t, z] = jnp.where(y_lo, 0.0, f_ym * scale)
+        c_yp[t, z] = jnp.where(y_hi, 0.0, f_yp * scale)
+        rhs[t, z] = strided(2, t, z) * scale
 
     rows(faces)
 
     def split(cell):
         plane = full_x * width
         rest = lax.rem(cell, plane)
-        return lax.div(cell, plane), lax.div(rest, width), lax.rem(rest, width)
+        x, y = lax.div(rest, width), lax.rem(rest, width)
+        spot = (s_at == lax.div(x, tiles)) & (y_at == y)
+        return lax.div(cell, plane), lax.rem(x, tiles), spot
 
     def solve(now, other):
-        def start(x):
-            now[x + 1] = rhs[x] * first
-            other[x + 1] = blank
+        def start(t, z):
+            now[t + 1, z] = rhs[t, z] * first
+            other[t + 1, z] = blank
 
         rows(start)
+        wrap(now)
 
         def sweep(src, dst, own, keep, step):
-            @pl.loop(0, full_x // UNROLL)
-            def _(block):
-                base = block * UNROLL
-                left = src[base]
-                here = src[base + 1]
-                for inner in range(UNROLL):
-                    x = base + inner
-                    right = src[x + 2]
-                    total = rhs[x] + c_xm[x] * left + c_xp[x] * right
-                    total += c_zm[x] * z_before(here) + c_zp[x] * z_after(here)
-                    total += c_ym[x] * y_before(here) + c_yp[x] * y_after(here)
-                    dst[x + 1] = own * here - keep * dst[x + 1] + step * total
-                    left, here = here, right
+            @pl.loop(0, tiles)
+            def _(t):
+                here = src[t + 1, 0]
+                for z in range(depth):
+                    total = rhs[t, z] + c_xm[t, z] * src[t, z] + c_xp[t, z] * src[t + 2, z]
+                    total += c_ym[t, z] * y_before(here) + c_yp[t, z] * y_after(here)
+                    if z > 0:
+                        total += c_zm[t, z] * before
+                    if z < depth - 1:
+                        after = src[t + 1, z + 1]
+                        total += c_zp[t, z] * after
+                    dst[t + 1, z] = own * here - keep * dst[t + 1, z] + step * total
+                    before, here = here, after
+
+            wrap(dst)
 
         @pl.loop(0, ITERS // 2)
         def _(pair):
@@ -272,35 +294,49 @@
             sweep(now, other, consts[0, k], consts[1, k], consts[2, k])
             sweep(other, now, consts[0, k + 1], consts[1, k + 1], consts[2, k + 1])
 
-    z, x, y = split(pump[0])
-    spot = (z_at == z) & (y_at == y)
-    rhs[x] = rhs[x] + jnp.where(spot, -PUMP_RATE * inv[x], 0.0)
+    z, t, spot = split(pump[0])
+    rhs[t, z] = rhs[t, z] + jnp.where(spot, -PUMP_RATE * inv[t, z], 0.0)
     solve(head_a, head_b)
 
-    def clear(x):
-        rhs[x] = blank
+    def clear(t, z):
+        rhs[t, z] = blank
 
     rows(clear)
 
     @pl.loop(0, ports.shape[1])
     def _(port):
-        z, x, y = split(ports[0, port])
-        spot = (z_at == z) & (y_at == y)
-        misfit = (head_a[x + 1] - heads[0, port]) * (1.0 / NOISE_VAR)
-        rhs[x] = rhs[x] + jnp.where(spot, misfit * inv[x], 0.0)
+        z, t, spot = split(ports[0, port])
+        misfit = (head_a[t + 1, z] - heads[0, port]) * (1.0 / NOISE_VAR)
+        rhs[t, z] = rhs[t, z] + jnp.where(spot, misfit * inv[t, z], 0.0)
 
     solve(adj_a, adj_b)
 
-    first_row = place[0]
-    for row in range(slab):
-        x = first_row + row
-        h, a = head_a[x + 1], adj_a[x + 1]
-        total = (a - adj_a[x]) * (h - head_a[x])
-        total += (a - adj_a[x + 2]) * (h - head_a[x + 2])
-        for move, mask in ((z_before, z_lo), (z_after, z_hi), (y_before, y_lo), (y_after, y_hi)):
-            total += (a - jnp.where(mask, 0.0, move(a))) * (h - jnp.where(mask, 0.0, move(h)))
-        terms[row] = -0.5 * cond[x + 1] * total
-    out[...] = jnp.swapaxes(terms[...], 0, 1)
+    def products(t, z):
+        h, a = head_a[t + 1, z], adj_a[t + 1, z]
+
+        def at(mask, h_near, a_near):
+            return (a - jnp.where(mask, 0.0, a_near)) * (h - jnp.where(mask, 0.0, h_near))
+
+        x_lo, x_hi = ends(t)
+        total = at(x_lo, head_a[t, z], adj_a[t, z])
+        total += at(x_hi, head_a[t + 2, z], adj_a[t + 2, z])
+        total += at(y_lo, y_before(h), y_before(a))
+        total += at(y_hi, y_after(h), y_after(a))
+        for near in (z - 1, z + 1):
+            if 0 <= near < depth:
+                total += (a - adj_a[t + 1, near]) * (h - head_a[t + 1, near])
+            else:
+                total += a * h
+        total = -0.5 * cond[t + 1, z] * total
+        at_rows = pl.ds(z * full_x + t, SUBLANES, stride=tiles)
+        for lane in range(width // LANES):
+            terms[lane, at_rows] = total[:, lane * LANES : (lane + 1) * LANES]
+
+    rows(products)
+    for z in range(depth):
+        own = pl.ds(pl.multiple_of(z * full_x + place[0], SUBLANES), slab)
+        for lane in range(width // LANES):
+            out[z, :, lane * LANES : (lane + 1) * LANES] = terms[lane, own]
 
 
 def shards(log_conductivity, storage, recharge, pump_cells, obs_cells, obs_heads):
@@ -308,14 +344,15 @@
     dom_count = lax.axis_size("dom")
     dom_index = lax.axis_index("dom")
     full_x = slab * dom_count
-    whole = pltpu.VMEM((full_x, depth, width), jnp.float32)
-    padded = pltpu.VMEM((full_x + 2, depth, width), jnp.float32)
+    tiles = full_x // SUBLANES
+    whole = pltpu.VMEM((tiles, depth, SUBLANES, width), jnp.float32)
+    padded = pltpu.VMEM((tiles + 2, depth, SUBLANES, width), jnp.float32)
     smem = pl.BlockSpec(memory_space=pltpu.SMEM)
     vmem = pl.BlockSpec(memory_space=pltpu.VMEM)
     chips = dom_count // 2
     cells = pl.pallas_call(
         functools.partial(gather_kernel, dom_count),
-        out_shape=jax.ShapeDtypeStruct((3, full_x, depth, width), jnp.float32),
+        out_shape=jax.ShapeDtypeStruct((3, width // LANES, full_x, depth, LANES), jnp.float32),
         in_specs=[vmem] * 3,
         out_specs=vmem,
         scratch_shapes=[pltpu.SemaphoreType.DMA((chips, 3))] * 2
@@ -330,7 +367,7 @@
         in_specs=[smem] * 5 + [vmem],
         out_specs=vmem,
         scratch_shapes=[padded] + [whole] * 8 + [padded] * 4
-        + [pltpu.VMEM((slab, depth, width), jnp.float32)],
+        + [pltpu.VMEM((width // LANES, depth * full_x, LANES), jnp.float32)],
         compiler_params=pltpu.CompilerParams(vmem_limit_bytes=VMEM_LIMIT),
     )(
         jnp.asarray(sweep_constants()),
@@ -338,7 +375,7 @@
         pump_cells,
         obs_cells,
         obs_heads,
-        cells,
+        cells.reshape(3, width // LANES, full_x * depth, LANES),
     )
     tests = lax.axis_size("test")
     layers = depth // tests

time: 75.6 us -> 79.5 us (1.052)
  Pallas kernels: 68.5 us -> 72.3 us
    pallas_call x1, Pallas kernels: 40.1 us -> 44 us  [shards(): pl.pallas_call(functools.partial(solve_kernel, slab), out_shape=jax.Shape...]
where the time goes in v3:
time: 79.5 us; the launch traced here: 79.2 us
  Pallas kernels  72.3 us (91%)
  matrix products  4.88 us (6%)
  between operations  1.37 us (2%)
    pallas_call x1, Pallas kernels, shards(): pl.pallas_call(functools.partial(solve_kernel, slab), out_shape=jax.Shape...  44 us
    pallas_call x1, Pallas kernels, shards(): pl.pallas_call(functools.partial(gather_kernel, dom_count), out_shape=jax...  16.2 us
    pallas_call x1, Pallas kernels, shards(): pl.pallas_call(functools.partial(reduce_kernel, tests, dom_count), out_sh...  12.2 us
    dot_general x1, matrix products, shards(): spectral = jnp.dot(full.reshape(-1, width), basis_y.T, precision=HIGHEST)  2.02 us

profile of v3, /device:TPU:0, one launch (start us, length us, event | category | flops | bytes accessed | tf_op | source)
XLA Modules:
  0.0 79.2 jit_solution(8131919379616051105)
XLA Ops:
  1.3 0.0 copy-start
  1.3 16.2 %shard_map.113 = f32[3,4,32,8,128]{4,3,2,1,0:T(8,128)} custom-call(f32[8,8,512]{2,1,0:T(8,128)} %conduct.1, f32[8,8,512]{2,1,0:T(8,128)} %storage.1, f32[8,8,512]{2,1,0:T(8,128)} %recharge.1), custom_call_target="tpu_custom_call" | custom-call | tf_op jit(solution)/shard_map/pallas_call | solution.py:353
  17.5 0.0 copy-start.1
  17.5 0.0 copy-start.3
  17.5 44.0 %shard_map.114.part = f32[8,8,512]{2,1,0:T(8,128)} custom-call(f32[3,32]{1,0:T(4,128)} %constant.19.clone.consts, s32[1]{0:T(128)} %bitcast.place, s32[1]{0:T(128)S(6)} %copy.13.pump, s32[1,32]{1,0:T(1,128)} %ports.1, f32[1,32]{1,0:T(1,128)} %heads.1, f32[3,4,256,128]{3,2,1,0:T(8,128)} %bitcast.20), custom_call_target="tpu_custom_call" | custom-call | tf_op jit(solution)/shard_map/pallas_call | solution.py:364
  61.5 0.0 copy-start.4
  61.5 12.2 %shard_map.115 = (f32[2,8,512]{2,1,0:T(8,128)}, f32[2,32,512]{2,1,0:T(8,128)}) custom-call(f32[8,8,512]{2,1,0:T(8,128)} %shard_map.114.part), custom_call_target="tpu_custom_call" | custom-call | tf_op jit(solution)/shard_map/pallas_call | solution.py:382
  73.7 0.0 copy-done
  73.7 2.0 %fusion.4 = f32[2,32,512]{2,1,0:T(8,128)S(1)} fusion(f32[2,32,512]{2,1,0:T(8,128)} %get-tuple-element.5, f32[512,512,1]{1,0,2:T(8,128)S(1)} %copy-done), kind=kOutput, calls=%fused_computation.6 | convolution fusion | flops 201326592 | bytes 1310720 | tf_op jit(solution)/shard_map/dot_general | solution.py:402
  75.7 0.0 copy-done.1
  75.7 0.0 copy-done.3
  75.7 0.0 copy-start.2
  75.7 1.0 %fusion = f32[2,32,512]{1,2,0:T(8,128)S(1)} fusion(f32[2,32,512]{2,1,0:T(8,128)S(1)} %fusion.4, f32[32,32,1]{1,0,2:T(8,128)S(1)} %copy-done.3, f32[32,512]{0,1:T(8,128)S(1)} %copy-done.1), kind=kOutput, calls=%fused_computation.1 | convolution fusion | flops 12615680 | bytes 331776 | tf_op jit(solution)/shard_map/fx,mxk->mfk/dot_general | solution.py:404
  76.8 0.0 copy-done.4
  76.8 0.6 convolution_bitcast_fusion.1
  77.4 1.3 %fusion.5 = f32[2,8,512]{2,1,0:T(8,128)} fusion(f32[2,8,512]{2,1,0:T(8,128)S(1)} %convolution_bitcast_fusion.1, f32[512,512,1]{1,0,2:T(8,128)S(1)} %copy-done), kind=kOutput, calls=%fused_computation.7 | convolution fusion | flops 50331648 | bytes 1114112 | tf_op jit(solution)/shard_map/dot_general | solution.py:407
  78.6 0.0 copy-done.2
  78.6 0.6 copy.14
Async XLA Ops:
  1.3 72.4 %copy-start = (f32[512,512,1]{1,0,2:T(8,128)S(1)}, f32[512,512,1]{1,0,2:T(8,128)}, u32[]{:S(2)}) copy-start(f32[512,512,1]{1,0,2:T(8,128)} %constant.26) | copy-start | bytes 3145732
  17.5 58.2 %copy-start.1 = (f32[32,512]{0,1:T(8,128)S(1)}, f32[32,512]{0,1:T(8,128)}, u32[]{:S(2)}) copy-start(f32[32,512]{0,1:T(8,128)} %constant.20.clone) | copy-start | bytes 196612
  17.5 58.2 %copy-start.3 = (f32[32,32,1]{1,0,2:T(8,128)S(1)}, f32[32,32,1]{1,0,2:T(8,128)}, u32[]{:S(2)}) copy-start(f32[32,32,1]{1,0,2:T(8,128)} %constant.27) | copy-start | bytes 12292
  61.5 15.3 %copy-start.4 = (f32[32,32]{1,0:T(8,128)S(1)}, f32[32,32]{1,0:T(8,128)}, u32[]{:S(2)}) copy-start(f32[32,32]{1,0:T(8,128)} %constant.21.clone) | copy-start | bytes 12292
  75.7 2.9 %copy-start.2 = (f32[2,8,512]{2,1,0:T(8,128)S(1)}, f32[2,8,512]{2,1,0:T(8,128)}, u32[]{:S(2)}) copy-start(f32[2,8,512]{2,1,0:T(8,128)} %get-tuple-element.8) | copy-start | bytes 98308

commit v4 on v2

--- a/solution.py
+++ b/solution.py
@@ -181,7 +181,7 @@
 
 def solve_kernel(
     slab, consts, place, pump, ports, heads, cells, out,
-    cond, inv, c_zm, c_zp, c_xm, c_xp, c_ym, c_yp, rhs, head_a, head_b, adj_a, adj_b, terms,
+    cond, scale, c_x, c_y, c_z, rhs, head_a, head_b, adj_a, adj_b, terms,
 ):
     full_x = cells.shape[1]
     depth, width = cells.shape[2:]
@@ -203,7 +203,7 @@
     def y_after(v):
         return pltpu.roll(v, width - 1, 1)
 
-    for field in (cond, head_a, head_b, adj_a, adj_b):
+    for field in (cond, scale, c_x, head_a, head_b, adj_a, adj_b):
         field[0] = blank
         field[full_x + 1] = blank
 
@@ -216,6 +216,7 @@
     def fill(x):
         cond[x + 1] = cells[0, x]
 
+    c_x[full_x] = blank
     rows(fill)
     first = 1.0 / (0.5 * (HIGH + LOW))
 
@@ -227,55 +228,72 @@
         f_xp = 0.5 * (here + cond[x + 2])
         f_ym = 0.5 * (here + jnp.where(y_lo, 0.0, y_before(here)))
         f_yp = 0.5 * (here + jnp.where(y_hi, 0.0, y_after(here)))
-        scale = 1.0 / (cells[1, x] + f_zm + f_zp + f_xm + f_xp + f_ym + f_yp)
-        inv[x] = scale
-        c_zm[x] = jnp.where(z_lo, 0.0, f_zm * scale)
-        c_zp[x] = jnp.where(z_hi, 0.0, f_zp * scale)
-        c_xm[x] = f_xm * scale
-        c_xp[x] = f_xp * scale
-        c_ym[x] = jnp.where(y_lo, 0.0, f_ym * scale)
-        c_yp[x] = jnp.where(y_hi, 0.0, f_yp * scale)
-        rhs[x] = cells[2, x] * scale
+        root = 1.0 / jnp.sqrt(cells[1, x] + f_zm + f_zp + f_xm + f_xp + f_ym + f_yp)
+        scale[x + 1] = root
+        c_x[x] = f_xm
+        c_y[x] = f_yp
+        c_z[x] = f_zp
+        rhs[x] = cells[2, x] * root
 
     rows(faces)
+
+    def couple(x):
+        root = scale[x + 1]
+        c_x[x] = c_x[x] * root * scale[x]
+        c_y[x] = jnp.where(y_hi, 0.0, c_y[x] * root * y_after(root))
+        c_z[x] = jnp.where(z_hi, 0.0, c_z[x] * root * z_after(root))
+
+    rows(couple)
 
     def split(cell):
         plane = full_x * width
         rest = lax.rem(cell, plane)
         return lax.div(cell, plane), lax.div(rest, width), lax.rem(rest, width)
 
-    def solve(now, other):
+    def solve(now, other, near_slab):
         def start(x):
             now[x + 1] = rhs[x] * first
             other[x + 1] = blank
 
         rows(start)
 
-        def sweep(src, dst, own, keep, step):
-            @pl.loop(0, full_x // UNROLL)
+        def sweep(src, dst, k):
+            own, keep, step = consts[0, k], consts[1, k], consts[2, k]
+            low, high = 0, full_x // UNROLL
+            if near_slab:
+                reach = ITERS - k
+                low = lax.div(jnp.maximum(place[0] - reach, 0), UNROLL)
+                high = lax.div(jnp.minimum(place[0] + slab + reach, full_x) + UNROLL - 1, UNROLL)
+
+            @pl.loop(low, high)
             def _(block):
                 base = block * UNROLL
-                left = src[base]
+                left = c_x[base] * src[base]
                 here = src[base + 1]
                 for inner in range(UNROLL):
                     x = base + inner
                     right = src[x + 2]
-                    total = rhs[x] + c_xm[x] * left + c_xp[x] * right
-                    total += c_zm[x] * z_before(here) + c_zp[x] * z_after(here)
-                    total += c_ym[x] * y_before(here) + c_yp[x] * y_after(here)
+                    face_x, face_y, face_z = c_x[x + 1], c_y[x], c_z[x]
+                    total = rhs[x] + left + face_x * right
+                    total += face_z * z_after(here) + z_before(face_z * here)
+                    total += face_y * y_after(here) + y_before(face_y * here)
                     dst[x + 1] = own * here - keep * dst[x + 1] + step * total
-                    left, here = here, right
+                    left, here = face_x * here, right
 
         @pl.loop(0, ITERS // 2)
         def _(pair):
-            k = 2 * pair
-            sweep(now, other, consts[0, k], consts[1, k], consts[2, k])
-            sweep(other, now, consts[0, k + 1], consts[1, k + 1], consts[2, k + 1])
+            sweep(now, other, 2 * pair)
+            sweep(other, now, 2 * pair + 1)
+
+        def unscale(x):
+            now[x + 1] = now[x + 1] * scale[x + 1]
+
+        rows(unscale)
 
     z, x, y = split(pump[0])
     spot = (z_at == z) & (y_at == y)
-    rhs[x] = rhs[x] + jnp.where(spot, -PUMP_RATE * inv[x], 0.0)
-    solve(head_a, head_b)
+    rhs[x] = rhs[x] + jnp.where(spot, -PUMP_RATE * scale[x + 1], 0.0)
+    solve(head_a, head_b, False)
 
     def clear(x):
         rhs[x] = blank
@@ -287,9 +305,9 @@
         z, x, y = split(ports[0, port])
         spot = (z_at == z) & (y_at == y)
         misfit = (head_a[x + 1] - heads[0, port]) * (1.0 / NOISE_VAR)
-        rhs[x] = rhs[x] + jnp.where(spot, misfit * inv[x], 0.0)
-
-    solve(adj_a, adj_b)
+        rhs[x] = rhs[x] + jnp.where(spot, misfit * scale[x + 1], 0.0)
+
+    solve(adj_a, adj_b, True)
 
     first_row = place[0]
     for row in range(slab):
@@ -329,7 +347,7 @@
         out_shape=jax.ShapeDtypeStruct((depth, slab, width), jnp.float32),
         in_specs=[smem] * 5 + [vmem],
         out_specs=vmem,
-        scratch_shapes=[padded] + [whole] * 8 + [padded] * 4
+        scratch_shapes=[padded] * 3 + [whole] * 3 + [padded] * 4
         + [pltpu.VMEM((slab, depth, width), jnp.float32)],
         compiler_params=pltpu.CompilerParams(vmem_limit_bytes=VMEM_LIMIT),
     )(
@@ -362,12 +380,12 @@
     weights = jnp.asarray(prior_table(freq_x, full_x, freq_y, width), jnp.float32)
     basis_x = jnp.asarray(basis_x, jnp.float32)
     basis_y = jnp.asarray(basis_y, jnp.float32)
-    spectral = jnp.dot(full.reshape(-1, width), basis_y.T, precision=HIGHEST)
+    spectral = jnp.dot(full.reshape(-1, width), basis_y.T, precision=lax.Precision.HIGH)
     spectral = spectral.reshape(layers, full_x, width)
     filtered = jnp.einsum("fx,mxk->mfk", basis_x, spectral, precision=HIGHEST) * weights
     own_x = lax.dynamic_slice_in_dim(basis_x, dom_index * slab, slab, axis=1)
     back = jnp.einsum("fx,mfk->mxk", own_x, filtered, precision=HIGHEST)
-    step_field = jnp.dot(back.reshape(-1, width), basis_y, precision=HIGHEST)
+    step_field = jnp.dot(back.reshape(-1, width), basis_y, precision=lax.Precision.HIGH)
     return gradient, step_field.reshape(layers, slab, width)
 
 

time: 75.6 us -> 74.3 us (0.983)
  matrix products: 4.88 us -> 4.12 us
    pallas_call x1, Pallas kernels: 40.1 us -> 37.7 us  [shards(): pl.pallas_call(functools.partial(solve_kernel, slab), out_shape=jax.Shape...]
    pallas_call x1, Pallas kernels: 12.2 us -> 14.1 us  [shards(): pl.pallas_call(functools.partial(reduce_kernel, tests, dom_count), out_sh...]
    dot_general x2, matrix products: 3.27 us -> 2.52 us  [the longest x1 1.51 us: shards(): jnp.dot(full.reshape(-1, width), basis_y.T, precision=lax.Precision.HIGH)]
where the time goes in v4:
time: 74.3 us; the launch traced here: 74.1 us
  Pallas kernels  68 us (92%)
  matrix products  4.12 us (6%)
  between operations  1.37 us (2%)
    pallas_call x1, Pallas kernels, shards(): pl.pallas_call(functools.partial(solve_kernel, slab), out_shape=jax.Shape...  37.7 us
    pallas_call x1, Pallas kernels, shards(): pl.pallas_call(functools.partial(gather_kernel, dom_count), out_shape=jax...  16.2 us
    pallas_call x1, Pallas kernels, shards(): pl.pallas_call(functools.partial(reduce_kernel, tests, dom_count), out_sh...  14.1 us
    dot_general x1, matrix products, shards(): jnp.dot(full.reshape(-1, width), basis_y.T, precision=lax.Precision.HIGH)  1.51 us

profile of v4, /device:TPU:0, one launch (start us, length us, event | category | flops | bytes accessed | tf_op | source)
XLA Modules:
  0.0 74.1 jit_solution(7355626496968922789)
XLA Ops:
  1.3 0.0 copy-start
  1.3 16.2 %shard_map.113.cells = f32[3,32,8,512]{3,2,1,0:T(8,128)} custom-call(f32[8,8,512]{2,1,0:T(8,128)} %conduct.1, f32[8,8,512]{2,1,0:T(8,128)} %storage.1, f32[8,8,512]{2,1,0:T(8,128)} %recharge.1), custom_call_target="tpu_custom_call" | custom-call | tf_op jit(solution)/shard_map/pallas_call | solution.py:334
  17.5 0.0 copy-start.1
  17.5 0.0 copy-start.3
  17.5 37.7 %shard_map.114.part = f32[8,8,512]{2,1,0:T(8,128)} custom-call(f32[3,32]{1,0:T(4,128)} %constant.19.clone.consts, s32[1]{0:T(128)} %bitcast.place, s32[1]{0:T(128)S(6)} %copy.13.pump, s32[1,32]{1,0:T(1,128)} %ports.1, f32[1,32]{1,0:T(1,128)} %heads.1, f32[3,32,8,512]{3,2,1,0:T(8,128)} %shard_map.113.cells), custom_call_target="tpu_custom_call" | custom-call | tf_op jit(solution)/shard_map/pallas_call | solution.py:345
  55.2 0.0 copy-start.4
  55.2 14.1 %shard_map.115 = (f32[2,8,512]{2,1,0:T(8,128)}, f32[2,32,512]{2,1,0:T(8,128)}) custom-call(f32[8,8,512]{2,1,0:T(8,128)} %shard_map.114.part), custom_call_target="tpu_custom_call" | custom-call | tf_op jit(solution)/shard_map/pallas_call | solution.py:363
  69.3 0.0 copy-done
  69.3 1.5 %fusion.4 = f32[2,32,512]{2,1,0:T(8,128)S(1)} fusion(f32[2,32,512]{2,1,0:T(8,128)} %get-tuple-element.5, f32[512,512,1]{1,0,2:T(8,128)S(1)} %copy-done), kind=kOutput, calls=%fused_computation.6 | convolution fusion | flops 100663296 | bytes 1310720 | tf_op jit(solution)/shard_map/dot_general | solution.py:383
  70.8 0.0 copy-done.1
  70.8 0.0 copy-done.3
  70.8 0.0 copy-start.2
  70.8 1.0 %fusion = f32[2,32,512]{1,2,0:T(8,128)S(1)} fusion(f32[2,32,512]{2,1,0:T(8,128)S(1)} %fusion.4, f32[32,32,1]{1,0,2:T(8,128)S(1)} %copy-done.3, f32[32,512]{0,1:T(8,128)S(1)} %copy-done.1), kind=kOutput, calls=%fused_computation.1 | convolution fusion | flops 12615680 | bytes 331776 | tf_op jit(solution)/shard_map/fx,mxk->mfk/dot_general | solution.py:385
  71.8 0.0 copy-done.4
  71.9 0.6 convolution_bitcast_fusion.1
  72.5 1.0 %fusion.5 = f32[2,8,512]{2,1,0:T(8,128)} fusion(f32[2,8,512]{2,1,0:T(8,128)S(1)} %convolution_bitcast_fusion.1, f32[512,512,1]{1,0,2:T(8,128)S(1)} %copy-done), kind=kOutput, calls=%fused_computation.7 | convolution fusion | flops 25165824 | bytes 1114112 | tf_op jit(solution)/shard_map/dot_general | solution.py:388
  73.5 0.0 copy-done.2
  73.5 0.6 copy.14
Async XLA Ops:
  1.3 68.0 %copy-start = (f32[512,512,1]{1,0,2:T(8,128)S(1)}, f32[512,512,1]{1,0,2:T(8,128)}, u32[]{:S(2)}) copy-start(f32[512,512,1]{1,0,2:T(8,128)} %constant.26) | copy-start | bytes 3145732
  17.5 53.3 %copy-start.1 = (f32[32,512]{0,1:T(8,128)S(1)}, f32[32,512]{0,1:T(8,128)}, u32[]{:S(2)}) copy-start(f32[32,512]{0,1:T(8,128)} %constant.20.clone) | copy-start | bytes 196612
  17.5 53.3 %copy-start.3 = (f32[32,32,1]{1,0,2:T(8,128)S(1)}, f32[32,32,1]{1,0,2:T(8,128)}, u32[]{:S(2)}) copy-start(f32[32,32,1]{1,0,2:T(8,128)} %constant.27) | copy-start | bytes 12292
  55.2 16.6 %copy-start.4 = (f32[32,32]{1,0:T(8,128)S(1)}, f32[32,32]{1,0:T(8,128)}, u32[]{:S(2)}) copy-start(f32[32,32]{1,0:T(8,128)} %constant.21.clone) | copy-start | bytes 12292
  70.8 2.6 %copy-start.2 = (f32[2,8,512]{2,1,0:T(8,128)S(1)}, f32[2,8,512]{2,1,0:T(8,128)}, u32[]{:S(2)}) copy-start(f32[2,8,512]{2,1,0:T(8,128)} %get-tuple-element.8) | copy-start | bytes 98308

commit v5 on v4

--- a/solution.py
+++ b/solution.py
@@ -18,7 +18,7 @@
 NUGGET = 1.0
 SMOOTH = 2.0
 HIGHEST = lax.Precision.HIGHEST
-UNROLL = 8
+UNROLL = 32
 MESH = pl.DeviceIdType.MESH
 VMEM_LIMIT = 56 * 1024 * 1024
 

time: 74.3 us -> 64.2 us (0.86)
  Pallas kernels: 68 us -> 57.9 us
    pallas_call x1, Pallas kernels: 37.7 us -> 29.5 us  [shards(): pl.pallas_call(functools.partial(solve_kernel, slab), out_shape=jax.Shape...]
    pallas_call x1, Pallas kernels: 14.1 us -> 12.2 us  [shards(): pl.pallas_call(functools.partial(reduce_kernel, tests, dom_count), out_sh...]
where the time goes in v5:
time: 64.2 us; the launch traced here: 64 us
  Pallas kernels  57.9 us (90%)
  matrix products  4.12 us (6%)
  between operations  1.37 us (2%)
    pallas_call x1, Pallas kernels, shards(): pl.pallas_call(functools.partial(solve_kernel, slab), out_shape=jax.Shape...  29.5 us
    pallas_call x1, Pallas kernels, shards(): pl.pallas_call(functools.partial(gather_kernel, dom_count), out_shape=jax...  16.2 us
    pallas_call x1, Pallas kernels, shards(): pl.pallas_call(functools.partial(reduce_kernel, tests, dom_count), out_sh...  12.2 us
    dot_general x1, matrix products, shards(): jnp.dot(full.reshape(-1, width), basis_y.T, precision=lax.Precision.HIGH)  1.51 us

profile of v5, /device:TPU:0, one launch (start us, length us, event | category | flops | bytes accessed | tf_op | source)
XLA Modules:
  0.0 64.0 jit_solution(12784542839823997740)
XLA Ops:
  1.3 0.0 copy-start
  1.3 16.2 %shard_map.113.cells = f32[3,32,8,512]{3,2,1,0:T(8,128)} custom-call(f32[8,8,512]{2,1,0:T(8,128)} %conduct.1, f32[8,8,512]{2,1,0:T(8,128)} %storage.1, f32[8,8,512]{2,1,0:T(8,128)} %recharge.1), custom_call_target="tpu_custom_call" | custom-call | tf_op jit(solution)/shard_map/pallas_call | solution.py:334
  17.5 0.0 copy-start.1
  17.5 0.0 copy-start.3
  17.5 29.5 %shard_map.114.part = f32[8,8,512]{2,1,0:T(8,128)} custom-call(f32[3,32]{1,0:T(4,128)} %constant.19.clone.consts, s32[1]{0:T(128)} %bitcast.place, s32[1]{0:T(128)S(6)} %copy.13.pump, s32[1,32]{1,0:T(1,128)} %ports.1, f32[1,32]{1,0:T(1,128)} %heads.1, f32[3,32,8,512]{3,2,1,0:T(8,128)} %shard_map.113.cells), custom_call_target="tpu_custom_call" | custom-call | tf_op jit(solution)/shard_map/pallas_call | solution.py:345
  47.0 0.0 copy-start.4
  47.0 12.2 %shard_map.115 = (f32[2,8,512]{2,1,0:T(8,128)}, f32[2,32,512]{2,1,0:T(8,128)}) custom-call(f32[8,8,512]{2,1,0:T(8,128)} %shard_map.114.part), custom_call_target="tpu_custom_call" | custom-call | tf_op jit(solution)/shard_map/pallas_call | solution.py:363
  59.2 0.0 copy-done
  59.2 1.5 %fusion.4 = f32[2,32,512]{2,1,0:T(8,128)S(1)} fusion(f32[2,32,512]{2,1,0:T(8,128)} %get-tuple-element.5, f32[512,512,1]{1,0,2:T(8,128)S(1)} %copy-done), kind=kOutput, calls=%fused_computation.6 | convolution fusion | flops 100663296 | bytes 1310720 | tf_op jit(solution)/shard_map/dot_general | solution.py:383
  60.7 0.0 copy-done.1
  60.7 0.0 copy-done.3
  60.8 0.0 copy-start.2
  60.8 1.0 %fusion = f32[2,32,512]{1,2,0:T(8,128)S(1)} fusion(f32[2,32,512]{2,1,0:T(8,128)S(1)} %fusion.4, f32[32,32,1]{1,0,2:T(8,128)S(1)} %copy-done.3, f32[32,512]{0,1:T(8,128)S(1)} %copy-done.1), kind=kOutput, calls=%fused_computation.1 | convolution fusion | flops 12615680 | bytes 331776 | tf_op jit(solution)/shard_map/fx,mxk->mfk/dot_general | solution.py:385
  61.8 0.0 copy-done.4
  61.8 0.6 convolution_bitcast_fusion.1
  62.4 1.0 %fusion.5 = f32[2,8,512]{2,1,0:T(8,128)} fusion(f32[2,8,512]{2,1,0:T(8,128)S(1)} %convolution_bitcast_fusion.1, f32[512,512,1]{1,0,2:T(8,128)S(1)} %copy-done), kind=kOutput, calls=%fused_computation.7 | convolution fusion | flops 25165824 | bytes 1114112 | tf_op jit(solution)/shard_map/dot_general | solution.py:388
  63.4 0.0 copy-done.2
  63.4 0.6 copy.14
Async XLA Ops:
  1.3 57.9 %copy-start = (f32[512,512,1]{1,0,2:T(8,128)S(1)}, f32[512,512,1]{1,0,2:T(8,128)}, u32[]{:S(2)}) copy-start(f32[512,512,1]{1,0,2:T(8,128)} %constant.26) | copy-start | bytes 3145732
  17.5 43.3 %copy-start.1 = (f32[32,512]{0,1:T(8,128)S(1)}, f32[32,512]{0,1:T(8,128)}, u32[]{:S(2)}) copy-start(f32[32,512]{0,1:T(8,128)} %constant.20.clone) | copy-start | bytes 196612
  17.5 43.2 %copy-start.3 = (f32[32,32,1]{1,0,2:T(8,128)S(1)}, f32[32,32,1]{1,0,2:T(8,128)}, u32[]{:S(2)}) copy-start(f32[32,32,1]{1,0,2:T(8,128)} %constant.27) | copy-start | bytes 12292
  47.0 14.8 %copy-start.4 = (f32[32,32]{1,0:T(8,128)S(1)}, f32[32,32]{1,0:T(8,128)}, u32[]{:S(2)}) copy-start(f32[32,32]{1,0:T(8,128)} %constant.21.clone) | copy-start | bytes 12292
  60.8 2.6 %copy-start.2 = (f32[2,8,512]{2,1,0:T(8,128)S(1)}, f32[2,8,512]{2,1,0:T(8,128)}, u32[]{:S(2)}) copy-start(f32[2,8,512]{2,1,0:T(8,128)} %get-tuple-element.8) | copy-start | bytes 98308
